TPU v7x, 32 devices: a whole 2x2x4 slice. The times are simulated.
32 devices in a mesh: rep: 16 (over z, y, core), shard: 2 (over x).
Axes of the slice: x: 2, y: 2, z: 4, core: 2. Of those that a mesh axis runs over, the one named last changes fastest.
Arguments:
- tokens: bfloat16 [16384, 1024], P(('rep', 'shard')), may hold values from -6 to 6
- segments: int32 [32, 512], P(('rep', 'shard')), may hold values from 0 to 2, as said below
- norm1_gain: bfloat16 [1024], P('shard'), may hold values from 0.099609375 to 1.8984375
- norm1_shift: bfloat16 [1024], P('shard'), may hold values from -3 to 3
- norm2_gain: bfloat16 [1024], P('shard'), may hold values from 0.099609375 to 1.8984375
- norm2_shift: bfloat16 [1024], P('shard'), may hold values from -3 to 3
- qkv_weight: bfloat16 [1024, 3072], P('shard'), may hold values from -0.1875 to 0.1875
- qkv_bias: bfloat16 [3072], P('shard'), may hold values from -3 to 3
- out_weight: bfloat16 [1024, 1024], P('shard'), may hold values from -0.5 to 0.5
- out_bias: bfloat16 [1024], P('shard'), may hold values from -2 to 2
- up_weight: bfloat16 [1024, 4096], P('shard'), may hold values from -0.1875 to 0.1875
- up_bias: bfloat16 [4096], P('shard'), may hold values from -3 to 3
- down_weight: bfloat16 [4096, 1024], P('shard'), may hold values from -0.09375 to 0.09375
- down_bias: bfloat16 [1024], P('shard'), may hold values from -2 to 2
- cotangent: bfloat16 [16384, 1024], P(('rep', 'shard')), may hold values from -6 to 6
Outputs:
- output: bfloat16 [16384, 1024], P(('rep', 'shard'))
- grad_tokens: bfloat16 [16384, 1024], P(('rep', 'shard'))
- grad_norm1_gain: float32 [1024], P('shard')
- grad_norm1_shift: float32 [1024], P('shard')
- grad_norm2_gain: float32 [1024], P('shard')
- grad_norm2_shift: float32 [1024], P('shard')
- grad_qkv_weight: float32 [1024, 3072], P('shard')
- grad_qkv_bias: float32 [3072], P('shard')
- grad_out_weight: float32 [1024, 1024], P('shard')
- grad_out_bias: float32 [1024], P('shard')
- grad_up_weight: float32 [1024, 4096], P('shard')
- grad_up_bias: float32 [4096], P('shard')
- grad_down_weight: float32 [4096, 1024], P('shard')
- grad_down_bias: float32 [1024], P('shard')
Inputs may be any that keep to these rules, and one draw needn't show every extreme that they name: `segments`: in each sequence the document numbers start at 0 and never fall, and each of the 3 documents appears; one document has exactly 256 tokens and each other one has 102 tokens or more.
All inputs are finite; a program needn't handle non-finite values.
Results may differ from a plain program's by a relative error of at most 0.011.
Values may be sent and summed in bfloat16 or wider, within the bound.
No kernel may reach another device: no remote copies, remote signals or barrier semaphores. Data moves between devices by JAX's collectives and lax.ppermute only.
A program may use at most 320 MiB of HBM per device.

v0:
```python
from functools import partial

import jax
import jax.numpy as jnp
from jax import lax
from jax.sharding import PartitionSpec as P

HEADS = 16
HD = 64
ROT = 16


epsilon = 1e-05
masked_score = -1e30


def layer_norm(values, norm_gain, norm_shift):
    average = jnp.mean(values, axis=-1, keepdims=True)
    centred = values - average
    spread = jnp.mean(centred * centred, axis=-1, keepdims=True)
    return centred * lax.rsqrt(spread + epsilon) * norm_gain + norm_shift


def rotary_tables(documents):
    length = documents.shape[0]
    places = jnp.arange(length, dtype=jnp.int32)
    before = jnp.sum((documents[None, :] < documents[:, None]).astype(jnp.int32), axis=1)
    offsets = (places - before).astype(jnp.float32)
    exponents = jnp.arange(0, ROT, 2, dtype=jnp.float32) / ROT
    inverse = 1.0 / 10000.0**exponents
    angles = offsets[:, None] * inverse[None, :]
    angles = jnp.concatenate([angles, angles], axis=-1)
    return (jnp.cos(angles), jnp.sin(angles))


def rotate(values, cosine, sine):
    turning = values[..., :ROT]
    halfway = ROT // 2
    turned = jnp.concatenate([-turning[..., halfway:], turning[..., :halfway]], axis=-1)
    moved = turning * cosine[:, None, :] + turned * sine[:, None, :]
    return jnp.concatenate([moved, values[..., ROT:]], axis=-1)


def contract(left, right, left_dim, right_dim):
    return lax.dot_general(
        left, right, (((left_dim,), (right_dim,)), ((), ())), preferred_element_type=jnp.float32
    )


def on_device(
    tokens,
    segments,
    norm1_gain,
    norm1_shift,
    norm2_gain,
    norm2_shift,
    qkv_weight,
    qkv_bias,
    out_weight,
    out_bias,
    up_weight,
    up_bias,
    down_weight,
    down_bias,
    cotangent,
):
    (
        gain_one,
        shift_one,
        gain_two,
        shift_two,
        qkv_full,
        qkv_bias_full,
        out_full,
        out_bias_full,
        up_full,
        up_bias_full,
        down_full,
        down_bias_full,
    ) = (
        lax.all_gather(norm1_gain, "shard", axis=0, tiled=True),
        lax.all_gather(norm1_shift, "shard", axis=0, tiled=True),
        lax.all_gather(norm2_gain, "shard", axis=0, tiled=True),
        lax.all_gather(norm2_shift, "shard", axis=0, tiled=True),
        lax.all_gather(qkv_weight, "shard", axis=0, tiled=True),
        lax.all_gather(qkv_bias, "shard", axis=0, tiled=True),
        lax.all_gather(out_weight, "shard", axis=0, tiled=True),
        lax.all_gather(out_bias, "shard", axis=0, tiled=True),
        lax.all_gather(up_weight, "shard", axis=0, tiled=True),
        lax.all_gather(up_bias, "shard", axis=0, tiled=True),
        lax.all_gather(down_weight, "shard", axis=0, tiled=True),
        lax.all_gather(down_bias, "shard", axis=0, tiled=True),
    )
    length, width = tokens.shape
    documents = segments[0]
    rows_all = tokens.astype(jnp.float32)
    norm_one, pull_one = jax.vjp(
        layer_norm, rows_all, gain_one.astype(jnp.float32), shift_one.astype(jnp.float32)
    )
    normed_one = norm_one.astype(jnp.bfloat16)
    mixed = jnp.dot(
        normed_one, qkv_full, preferred_element_type=jnp.float32
    ) + qkv_bias_full.astype(jnp.float32)
    mixed = mixed.reshape(length, 3, HEADS, HD)
    cosine, sine = rotary_tables(documents)
    query_turned, pull_query = jax.vjp(
        lambda values_in: rotate(values_in, cosine, sine), mixed[:, 0]
    )
    key_turned, pull_key = jax.vjp(lambda values_in: rotate(values_in, cosine, sine), mixed[:, 1])
    queries = query_turned.astype(jnp.bfloat16)
    keys = key_turned.astype(jnp.bfloat16)
    values = mixed[:, 2].astype(jnp.bfloat16)
    block_rows = min(512, length)
    block_count = length // block_rows
    scale = HD ** (-0.5)
    places = jnp.arange(length, dtype=jnp.int32)
    query_blocks = queries.reshape(block_count, block_rows, HEADS, HD)
    starts = jnp.arange(block_count, dtype=jnp.int32) * block_rows

    def scores_for(query_block, start):
        raw_scores = (
            jnp.einsum("qhd,khd->hqk", query_block, keys, preferred_element_type=jnp.float32)
            * scale
        )
        rows_here = start + jnp.arange(block_rows, dtype=jnp.int32)
        allowed = (documents[:, None] == documents[None, :]) & (
            places[None, :] <= rows_here[:, None]
        )
        return jnp.where(allowed[None], raw_scores, masked_score)

    def forward_block(entry):
        query_block, start = entry
        scores = scores_for(query_block, start)
        highest_score = jnp.max(scores, axis=-1, keepdims=True)
        weights = jnp.exp(scores - highest_score)
        total = jnp.sum(weights, axis=-1, keepdims=True)
        probs = weights / total
        context_block = jnp.einsum(
            "hqk,khd->qhd", probs.astype(jnp.bfloat16), values, preferred_element_type=jnp.float32
        )
        log_total = highest_score[..., 0] + jnp.log(total[..., 0])
        return (context_block, log_total)

    context_blocks, log_totals = lax.map(forward_block, (query_blocks, starts))
    context = context_blocks.reshape(length, width).astype(jnp.bfloat16)
    attn_result = jnp.dot(
        context, out_full, preferred_element_type=jnp.float32
    ) + out_bias_full.astype(jnp.float32)
    norm_two, pull_two = jax.vjp(
        layer_norm, rows_all, gain_two.astype(jnp.float32), shift_two.astype(jnp.float32)
    )
    normed_two = norm_two.astype(jnp.bfloat16)
    hidden = jnp.dot(normed_two, up_full, preferred_element_type=jnp.float32) + up_bias_full.astype(
        jnp.float32
    )
    active_value, pull_gelu = jax.vjp(partial(jax.nn.gelu, approximate=False), hidden)
    active = active_value.astype(jnp.bfloat16)
    ffn_result = jnp.dot(
        active, down_full, preferred_element_type=jnp.float32
    ) + down_bias_full.astype(jnp.float32)
    output = (rows_all + attn_result + ffn_result).astype(jnp.bfloat16)
    grad_rows = cotangent.astype(jnp.float32)
    grad_down_bias = jnp.sum(grad_rows, axis=0)
    grad_down = contract(active, cotangent, 0, 0)
    grad_out = contract(context, cotangent, 0, 0)
    grad_active = contract(cotangent, down_full, 1, 1)
    grad_hidden = pull_gelu(grad_active)[0].astype(jnp.bfloat16)
    grad_up_bias = jnp.sum(grad_hidden.astype(jnp.float32), axis=0)
    grad_up = contract(normed_two, grad_hidden, 0, 0)
    grad_normed_two = contract(grad_hidden, up_full, 1, 1)
    grad_context = contract(cotangent, out_full, 1, 1).astype(jnp.bfloat16)
    grad_context_blocks = grad_context.reshape(block_count, block_rows, HEADS, HD)

    def backward_block(carry, entry):
        grad_keys, grad_values = carry
        query_block, grad_block, log_total, start = entry
        scores = scores_for(query_block, start)
        probs = jnp.exp(scores - log_total[..., None])
        grad_probs = jnp.einsum(
            "qhd,khd->hqk", grad_block, values, preferred_element_type=jnp.float32
        )
        inner = jnp.sum(probs * grad_probs, axis=-1, keepdims=True)
        grad_scores = (probs * (grad_probs - inner)).astype(jnp.bfloat16)
        grad_query_block = (
            jnp.einsum("hqk,khd->qhd", grad_scores, keys, preferred_element_type=jnp.float32)
            * scale
        )
        grad_keys = (
            grad_keys
            + jnp.einsum(
                "hqk,qhd->khd", grad_scores, query_block, preferred_element_type=jnp.float32
            )
            * scale
        )
        grad_values = grad_values + jnp.einsum(
            "hqk,qhd->khd",
            probs.astype(jnp.bfloat16),
            grad_block,
            preferred_element_type=jnp.float32,
        )
        return ((grad_keys, grad_values), grad_query_block)

    empty_heads = jnp.zeros((length, HEADS, HD), jnp.float32)
    (grad_keys, grad_values), grad_queries = lax.scan(
        backward_block,
        (empty_heads, empty_heads),
        (query_blocks, grad_context_blocks, log_totals, starts),
    )
    grad_queries = grad_queries.reshape(length, HEADS, HD)
    grad_mixed = jnp.stack(
        [pull_query(grad_queries)[0], pull_key(grad_keys)[0], grad_values], axis=1
    )
    grad_mixed = grad_mixed.reshape(length, 3 * width).astype(jnp.bfloat16)
    grad_qkv_bias = jnp.sum(grad_mixed.astype(jnp.float32), axis=0)
    grad_qkv = contract(normed_one, grad_mixed, 0, 0)
    grad_normed_one = contract(grad_mixed, qkv_full, 1, 1)
    grad_input_one, grad_gain_one, grad_shift_one = pull_one(grad_normed_one)
    grad_input_two, grad_gain_two, grad_shift_two = pull_two(grad_normed_two)
    grad_tokens = (grad_rows + grad_input_one + grad_input_two).astype(jnp.bfloat16)
    owned = (
        lax.psum_scatter(
            grad_gain_one.astype(jnp.bfloat16), "shard", scatter_dimension=0, tiled=True
        ).astype(jnp.float32),
        lax.psum_scatter(
            grad_shift_one.astype(jnp.bfloat16), "shard", scatter_dimension=0, tiled=True
        ).astype(jnp.float32),
        lax.psum_scatter(
            grad_gain_two.astype(jnp.bfloat16), "shard", scatter_dimension=0, tiled=True
        ).astype(jnp.float32),
        lax.psum_scatter(
            grad_shift_two.astype(jnp.bfloat16), "shard", scatter_dimension=0, tiled=True
        ).astype(jnp.float32),
        lax.psum_scatter(
            grad_qkv.astype(jnp.bfloat16), "shard", scatter_dimension=0, tiled=True
        ).astype(jnp.float32),
        lax.psum_scatter(
            grad_qkv_bias.astype(jnp.bfloat16), "shard", scatter_dimension=0, tiled=True
        ).astype(jnp.float32),
        lax.psum_scatter(
            grad_out.astype(jnp.bfloat16), "shard", scatter_dimension=0, tiled=True
        ).astype(jnp.float32),
        lax.psum_scatter(
            grad_down_bias.astype(jnp.bfloat16), "shard", scatter_dimension=0, tiled=True
        ).astype(jnp.float32),
        lax.psum_scatter(
            grad_up.astype(jnp.bfloat16), "shard", scatter_dimension=0, tiled=True
        ).astype(jnp.float32),
        lax.psum_scatter(
            grad_up_bias.astype(jnp.bfloat16), "shard", scatter_dimension=0, tiled=True
        ).astype(jnp.float32),
        lax.psum_scatter(
            grad_down.astype(jnp.bfloat16), "shard", scatter_dimension=0, tiled=True
        ).astype(jnp.float32),
        lax.psum_scatter(
            grad_down_bias.astype(jnp.bfloat16), "shard", scatter_dimension=0, tiled=True
        ).astype(jnp.float32),
    )
    totals = lax.psum(
        (
            owned[0],
            owned[1],
            owned[2],
            owned[3],
            owned[4],
            owned[5],
            owned[6],
            owned[7],
            owned[8],
            owned[9],
            owned[10],
            owned[11],
        ),
        "rep",
    )
    return (
        output,
        grad_tokens,
        totals[0],
        totals[1],
        totals[2],
        totals[3],
        totals[4],
        totals[5],
        totals[6],
        totals[7],
        totals[8],
        totals[9],
        totals[10],
        totals[11],
    )


def solution(mesh):
    return jax.shard_map(
        on_device,
        mesh=mesh,
        in_specs=(
            P(("rep", "shard"), None),
            P(("rep", "shard"), None),
            P("shard"),
            P("shard"),
            P("shard"),
            P("shard"),
            P("shard", None),
            P("shard"),
            P("shard", None),
            P("shard"),
            P("shard", None),
            P("shard"),
            P("shard", None),
            P("shard"),
            P(("rep", "shard"), None),
        ),
        out_specs=(
            P(("rep", "shard"), None),
            P(("rep", "shard"), None),
            P("shard"),
            P("shard"),
            P("shard"),
            P("shard"),
            P("shard", None),
            P("shard"),
            P("shard", None),
            P("shard"),
            P("shard", None),
            P("shard"),
            P("shard", None),
            P("shard"),
        ),
        check_vma=False,
    )
```

profile of v0, /device:TPU:0, one launch (start us, length us, event | category | flops | bytes accessed | tf_op | source)
XLA Modules:
  0.0 1183.0 jit_solution(9574433456725687727)
XLA Ops:
  10.7 5.3 all-gather.2
  16.0 4.3 all-gather.1
  20.4 4.4 all-gather
  26.1 19.3 %all-gather.14.cloned.1.call-done = bf16[1024,1024]{1,0:T(8,128)(2,1)} async-done(((bf16[512,1024]{1,0:T(8,128)(2,1)}), bf16[1024,1024]{1,0:T(8,128)(2,1)}) %all-gather.14.cloned.1.call-update) | async-done | bytes 2097168 | tf_op jit(solution)/shard_map/all_gather | solution.py:87
  51.0 76.4 %all-gather.12.cloned.1.call-done = bf16[1024,3072]{1,0:T(8,128)(2,1)} async-done(((bf16[512,3072]{1,0:T(8,128)(2,1)}), bf16[1024,3072]{1,0:T(8,128)(2,1)}) %all-gather.12.cloned.1.call-update) | async-done | bytes 6291472 | tf_op jit(solution)/shard_map/all_gather | solution.py:85
  127.4 8.3 convolution_add_fusion
  135.7 7.2 copy.44
  147.1 7.3 fusion.66
  154.4 8.3 fusion
  162.7 9.2 fusion.36
  175.5 11.9 %multiply_reduce_fusion = (f32[16,512]{1,0:T(8,128)S(1)}, f32[16,512,512]{1,2,0:T(8,128)}) fusion(f32[16,512,512]{1,2,0:T(8,128)} %get-tuple-element.127, f32[16,512]{1,0:T(8,128)S(1)} %log_add_fusion, bf16[512,16,64]{0,2,1:T(8,128)(2,1)S(1)} %bitcast.66, f32[512,3,16,64]{0,3,2,1:T(8,128)} %bitcast.65), kind=kOutput, calls=%fused_computation.1 | convolution fusion | flops 549445632 | bytes 35717120 | tf_op jit(solution)/shard_map/while/body/eval_jaxpr/qhd,khd->hqk/dot_general | solution.py:179
  187.5 12.0 %multiply_convert_fusion = bf16[16,512,512]{1,2,0:T(8,128)(2,1)S(1)} fusion(f32[16,512,512]{1,2,0:T(8,128)} %get-tuple-element.129, f32[16,512,512]{1,2,0:T(8,128)} %get-tuple-element.127, f32[16,512]{1,0:T(8,128)S(1)} %get-tuple-element.128, f32[16,512]{1,0:T(8,128)S(1)} %log_add_fusion), kind=kLoop, calls=%fused_computation | loop fusion | flops 16777216 | bytes 42008576 | tf_op jit(solution)/shard_map/while/body/eval_jaxpr/convert_element_type | solution.py:183
  202.9 5.6 multiply_bitcast_fusion.1
  215.5 5.0 fusion.33
  224.3 5.9 convolution_convert_fusion.2
  239.6 4.3 all_gather.45
  244.0 11.8 fusion.53
  255.8 82.6 %all-gather.18.cloned.1.call-done = bf16[4096,1024]{1,0:T(8,128)(2,1)} async-done(((bf16[2048,1024]{1,0:T(8,128)(2,1)}), bf16[4096,1024]{1,0:T(8,128)(2,1)}) %all-gather.18.cloned.1.call-update) | async-done | bytes 8388624 | tf_op jit(solution)/shard_map/all_gather | solution.py:91
  338.4 27.4 %fusion.61 = (bf16[4096]{0:T(1024)(128)(2,1)S(1)}, bf16[512,4096]{1,0:T(8,128)(2,1)S(1)}, f32[512,4096]{1,0:T(8,128)}) fusion(f32[512,4096]{1,0:T(8,128)} %fusion.53, f32[4096]{0:T(1024)S(1)} %convert_element_type.175, bf16[512,1024]{1,0:T(8,128)(2,1)S(1)} %copy-done.7, bf16[4096,1024]{1,0:T(8,128)(2,1)} %all-gather.18.cloned.1.call-done), kind=kOutput, calls=%fused_computation.126 | convolution fusion | flops 4450152448 | bytes 30433280 | tf_op jit(solution)/shard_map/dot_general | solution.py:45
  367.8 7.4 convolution_convert_fusion.1
  375.4 9.8 multiply_convert_fusion.1
  385.2 9.0 convolution_convert_fusion
  394.9 4.3 all-gather.6
  399.2 4.4 all-gather.3
  406.4 8.4 fusion.68
  414.8 6.4 fusion.60
  424.4 7.7 all-reduce.16
  436.5 7.0 fusion.67
  445.9 7.0 reduce-scatter.5.cloned.1.call-done
  452.9 101.6 %reduce-scatter.9.cloned.1.call-done = bf16[512,4096]{1,0:T(8,128)(2,1)} async-done(((bf16[1024,4096]{1,0:T(8,128)(2,1)}), bf16[512,4096]{1,0:T(8,128)(2,1)}) %reduce-scatter.9.cloned.1.call-update) | async-done | bytes 4194320 | tf_op jit(solution)/shard_map/reduce_scatter | solution.py:245
  554.5 102.2 %reduce-scatter.11.cloned.1.call-done = bf16[2048,1024]{1,0:T(8,128)(2,1)} async-done(((bf16[4096,1024]{1,0:T(8,128)(2,1)}), bf16[2048,1024]{1,0:T(8,128)(2,1)}) %reduce-scatter.11.cloned.1.call-update) | async-done | bytes 4194320 | tf_op jit(solution)/shard_map/reduce_scatter | solution.py:251
  656.7 518.6 %all-reduce.18 = (f32[512]{0:T(512)}, f32[512]{0:T(512)}, f32[512]{0:T(512)}, f32[512]{0:T(512)}, f32[512,3072]{1,0:T(8,128)}, /*index=5*/f32[1536]{0:T(1024)}, ...) all-reduce(f32[512]{0:T(512)S(1)} %dynamic-slice_convert_fusion.6, ...), channel_id=1, replica_groups=mesh['rep'=16,'shard'=2] {'rep'}, use_global_device_ids=true, to_apply=%region_12.13 | all-reduce | flops 6297600 | bytes 37797888 | tf_op jit(solution)/shard_map/psum | solution.py:258
  (172 shorter events, 55.8 us)
Async XLA Ops:
  7.2 38.2 %all-gather.14.cloned.1.call-start = ((), (), s32[]{:S(2)}) async-start(), calls=%async_computation.5 | async-start | bytes 3145728 | tf_op jit(solution)/shard_map/all_gather | solution.py:87
  7.9 119.5 %all-gather.12.cloned.1.call-start = ((), (), s32[]{:S(2)}) async-start(), calls=%async_computation.4 | async-start | bytes 9437184 | tf_op jit(solution)/shard_map/all_gather | solution.py:85
  8.7 7.3 copy-start.29
  8.7 11.6 copy-start.30
  8.7 235.3 %all-gather.16.cloned.1.call-start = ((), (), s32[]{:S(2)}) async-start(), calls=%async_computation.6 | async-start | bytes 12582912 | tf_op jit(solution)/shard_map/all_gather | solution.py:89
  9.4 36.0 %copy-start.6 = (bf16[512,1024]{1,0:T(8,128)(2,1)S(1)}, bf16[512,1024]{1,0:T(8,128)(2,1)}, u32[]{:S(2)}) copy-start(bf16[512,1024]{1,0:T(8,128)(2,1)} %param.29) | copy-start | bytes 3145732
  9.5 329.0 %all-gather.18.cloned.1.call-start = ((), (), s32[]{:S(2)}) async-start(), calls=%async_computation.7 | async-start | bytes 12582912 | tf_op jit(solution)/shard_map/all_gather | solution.py:91
  10.0 435.9 %reduce-scatter.7.cloned.1.call-start = ((), (), s32[]{:S(2)}) async-start(), calls=%async_computation.9 | async-start | bytes 3145728 | tf_op jit(solution)/shard_map/reduce_scatter | solution.py:239
  10.7 135.9 %copy-start.18 = (f32[512,16]{0,1:T(8,128)}, f32[512,16]{0,1:T(8,128)S(1)}, u32[]{:S(2)}) copy-start(f32[512,16]{0,1:T(8,128)S(1)} %get-tuple-element.122) | copy-start | bytes 98308
  20.4 107.0 %copy-start.26 = (f32[2,1,512]{2,1,0:T(1,128)}, f32[2,1,512]{2,1,0:T(1,128)S(1)}, u32[]{:S(2)}) copy-start(f32[2,1,512]{2,1,0:T(1,128)S(1)} %convert_element_type.207) | copy-start | bytes 12292
  25.2 24.1 %copy-start.22 = (f32[512]{0:T(512)}, f32[512]{0:T(512)S(1)}, u32[]{:S(2)}) copy-start(f32[512]{0:T(512)S(1)} %fusion.28) | copy-start | bytes 6148
  51.0 124.6 %copy-start.4 = (bf16[512,1024]{0,1:T(8,128)(2,1)}, bf16[512,1024]{0,1:T(8,128)(2,1)S(1)}, u32[]{:S(2)}) copy-start(bf16[512,1024]{0,1:T(8,128)(2,1)S(1)} %copy.46) | copy-start | bytes 3145732
  146.3 8.1 copy-start.9
  146.4 8.0 copy-start.11
  146.8 7.5 copy-start.15
  162.7 24.8 %copy-start.17 = (f32[16,512]{1,0:T(8,128)}, f32[16,512]{1,0:T(8,128)S(1)}, u32[]{:S(2)}) copy-start(f32[16,512]{1,0:T(8,128)S(1)} %log_add_fusion) | copy-start | bytes 98308
  187.4 265.5 %reduce-scatter.5.cloned.1.call-start = ((), (), s32[]{:S(2)}) async-start(), calls=%async_computation.8 | async-start | bytes 9437184 | tf_op jit(solution)/shard_map/reduce_scatter | solution.py:233
  187.5 12.0 %copy-start.12 = (bf16[512,16,48]{0,2,1:T(8,128)(2,1)S(1)}, bf16[512,16,48]{0,2,1:T(8,128)(2,1)}, u32[]{:S(2)}) copy-start(bf16[512,16,48]{0,2,1:T(8,128)(2,1)} %copy-done.11) | copy-start | bytes 2359300
  187.5 12.0 %copy-start.16 = (bf16[512,16,16]{0,2,1:T(8,128)(2,1)S(1)}, bf16[512,16,16]{0,2,1:T(8,128)(2,1)}, u32[]{:S(2)}) copy-start(bf16[512,16,16]{0,2,1:T(8,128)(2,1)} %copy-done.15) | copy-start | bytes 786436
  202.9 5.6 copy-start.3
  202.9 12.5 %slice-start = ((s8[16777216]{0:T(1024)(128)(4,1)}), s8[4194304]{0:T(1024)(128)(4,1)S(1)}, s32[]{:S(2)}) async-start(s8[16777216]{0:T(1024)(128)(4,1)} %bitcast.61), calls=%async_computation.12 | async-start | bytes 8388608
  202.9 12.5 %slice-start.1 = ((s8[16777216]{0:T(1024)(128)(4,1)}), s8[4194304]{0:T(1024)(128)(4,1)S(1)}, s32[]{:S(2)}) async-start(s8[16777216]{0:T(1024)(128)(4,1)} %bitcast.61), calls=%async_computation.13 | async-start | bytes 8388608
  202.9 12.5 %slice-start.2 = ((s8[16777216]{0:T(1024)(128)(4,1)}), s8[4194304]{0:T(1024)(128)(4,1)S(1)}, s32[]{:S(2)}) async-start(s8[16777216]{0:T(1024)(128)(4,1)} %bitcast.61), calls=%async_computation.14 | async-start | bytes 8388608
  230.3 9.4 copy-start.24
  230.3 324.2 %reduce-scatter.9.cloned.1.call-start = ((), (), s32[]{:S(2)}) async-start(), calls=%async_computation.10 | async-start | bytes 12582912 | tf_op jit(solution)/shard_map/reduce_scatter | solution.py:245
  244.0 94.4 %copy-start.7 = (bf16[512,1024]{1,0:T(8,128)(2,1)S(1)}, bf16[512,1024]{1,0:T(8,128)(2,1)}, u32[]{:S(2)}) copy-start(bf16[512,1024]{1,0:T(8,128)(2,1)} %param.29) | copy-start | bytes 3145732
  375.2 281.5 %reduce-scatter.11.cloned.1.call-start = ((), (), s32[]{:S(2)}) async-start(), calls=%async_computation.11 | async-start | bytes 12582912 | tf_op jit(solution)/shard_map/reduce_scatter | solution.py:251
  394.2 9.6 copy-start.38
  406.4 8.4 copy-start.14
  414.8 6.5 copy-start.23
  436.5 7.0 copy-start.35
  436.5 7.0 copy-start.37
  (22 other events, 55.4 us)
Sparse Core Ops, SparseCore 0:
  9.6 35.8 all-gather.13
  47.0 80.3 all-gather.11
  128.9 103.9 all-gather.15
  234.4 104.0 all-gather.17
  340.5 31.8 reduce-scatter.6
  375.2 77.6 reduce-scatter.4
  455.2 99.2 reduce-scatter.8
  557.4 99.2 reduce-scatter.10
where the time goes:
time: 1200 us; the launch traced here: 1180 us
  blocking collectives  562 us (47%)
  waiting for transfers between devices  392 us (33%)
  matrix products  142 us (12%)
  other arithmetic  44.8 us (4%)
  local copies, waits for them, and re-layouts  24.9 us (2%)
  between operations  17 us (1%)
    psum x1, blocking collectives, on_device(): lax.psum((owned[0], owned[1], owned[2], owned[3], owned[4], owned[5], own...  519 us
    reduce_scatter x1, waiting for transfers between devices, on_device(): lax.psum_scatter(grad_down.astype(jnp.bfloat16), 'shard', scatter_dimensi...  102 us
    reduce_scatter x1, waiting for transfers between devices, on_device(): lax.psum_scatter(grad_up.astype(jnp.bfloat16), 'shard', scatter_dimension...  102 us
    all_gather x1, waiting for transfers between devices, on_device(): lax.all_gather(down_weight, 'shard', axis=0, tiled=True)  82.6 us
    all_gather x1, waiting for transfers between devices, on_device(): lax.all_gather(qkv_weight, 'shard', axis=0, tiled=True)  76.4 us
    dot_general x8, matrix products, contract(): lax.dot_general(left, right, (((left_dim,), (right_dim,)), ((), ())), pre...  70.9 us
  transfers between devices with their start and end apart: 8, of which 6 were waited for; matrix products, arithmetic and copies ran while one was open for 17% of the time, Pallas kernels for 0%

commit v1 on v0

v1 whole, which is shorter than its diff:
```python
import jax
import jax.numpy as jnp
from jax import lax
from jax.sharding import PartitionSpec as P

HEADS = 16
HD = 64
ROT = 16

EPSILON = 1e-05
MASKED = -1e30
BF = jnp.bfloat16
F32 = jnp.float32


def dot(left, right, left_dim=1, right_dim=0, kind=F32):
    return lax.dot_general(
        left, right, (((left_dim,), (right_dim,)), ((), ())), preferred_element_type=kind
    )


def rotary_tables(documents):
    length = documents.shape[0]
    places = jnp.arange(length, dtype=jnp.int32)
    before = jnp.sum((documents[None, :] < documents[:, None]).astype(jnp.int32), axis=1)
    offsets = (places - before).astype(F32)
    exponents = jnp.arange(0, ROT, 2, dtype=F32) / ROT
    inverse = 1.0 / 10000.0**exponents
    angles = offsets[:, None] * inverse[None, :]
    angles = jnp.concatenate([angles, angles], axis=-1)
    return jnp.cos(angles), jnp.sin(angles)


def rotate(values, cosine, sine):
    turning = values[..., :ROT]
    halfway = ROT // 2
    turned = jnp.concatenate([-turning[..., halfway:], turning[..., :halfway]], axis=-1)
    moved = turning * cosine[:, :, None, :] + turned * sine[:, :, None, :]
    return jnp.concatenate([moved, values[..., ROT:]], axis=-1)


def build(reps):
    bits = reps.bit_length() - 1
    upper = list(range(2, bits))

    def flip(array, bit):
        return lax.ppermute(array, "rep", [(i, i ^ (1 << bit)) for i in range(reps)])

    def flip_x(array):
        return lax.ppermute(array, "shard", [(0, 1), (1, 0)])

    def on_device(
        tokens, segments, norm1_gain, norm1_shift, norm2_gain, norm2_shift, qkv_weight, qkv_bias,
        out_weight, out_bias, up_weight, up_bias, down_weight, down_bias, cotangent,
    ):
        half, width = out_weight.shape
        length = tokens.shape[0]
        ff_half = down_weight.shape[0]
        xi = lax.axis_index("shard")
        ri = lax.axis_index("rep")
        rbit = [(ri >> b) & 1 for b in range(bits)]
        ci, yi = rbit[0], rbit[1]

        def ordered(bit, own, other, axis=0):
            return jnp.where(
                bit == 0,
                jnp.concatenate([own, other], axis),
                jnp.concatenate([other, own], axis),
            )

        def pick(array, index, axis):
            return lax.dynamic_index_in_dim(array, index, axis, keepdims=False)

        heads_core = half // 2
        up_own = pick(up_weight.reshape(half, 2, 2, ff_half // 2), ci, 2).reshape(half, ff_half)
        down_own = pick(down_weight.reshape(2, ff_half // 2, width), ci, 0)
        qkv_own = pick(qkv_weight.reshape(half, 3, 2, 2, heads_core), ci, 3).reshape(half, 3 * half)
        out_own = pick(out_weight.reshape(2, heads_core, width), ci, 0)

        def fetch(own):
            rows = own.shape[0] // 2
            part = lax.dynamic_slice_in_dim(own, yi * rows, rows, 0)
            first = flip_x(part)
            second = flip(first, 1)
            return first, second

        def whole(own, pair):
            return ordered(xi, own, ordered(yi, *pair))

        small_own = jnp.concatenate(
            [norm1_gain, norm1_shift, norm2_gain, norm2_shift, out_bias, down_bias, qkv_bias, up_bias]
        )
        small_other = flip_x(small_own)
        tokens_other = flip(tokens, 0)
        cot_other = flip(cotangent, 0)
        segments_other = flip(segments, 0)
        up_pair = fetch(up_own)
        down_pair = fetch(down_own)
        qkv_pair = fetch(qkv_own)
        out_pair = fetch(out_own)

        low = jnp.where(xi == 0, small_own, small_other).astype(F32)
        high = jnp.where(xi == 0, small_other, small_own).astype(F32)
        full = []
        at = 0
        for size in [half] * 6 + [qkv_bias.shape[0], ff_half]:
            full.append(jnp.concatenate([low[at : at + size], high[at : at + size]]))
            at += size
        gain_one, shift_one, gain_two, shift_two, out_b, down_b, qkv_b, up_b = full
        qkv_bc = pick(qkv_b.reshape(3, 2, 2, heads_core), ci, 2).reshape(3 * half)
        up_bc = pick(up_b.reshape(2, 2, ff_half // 2), ci, 1).reshape(ff_half)

        both = jnp.concatenate([tokens, tokens_other], 0)
        cot = jnp.concatenate([cotangent, cot_other], 0)
        rows = both.astype(F32)
        average = jnp.mean(rows, axis=-1, keepdims=True)
        centred = rows - average
        spread = lax.rsqrt(jnp.mean(centred * centred, axis=-1, keepdims=True) + EPSILON)
        unit = centred * spread
        normed_one = (unit * gain_one + shift_one).astype(BF)
        normed_two = (unit * gain_two + shift_two).astype(BF)

        def split(array, axis):
            size = array.shape[axis] // 2
            own = lax.dynamic_slice_in_dim(array, xi * size, size, axis)
            other = lax.dynamic_slice_in_dim(array, (1 - xi) * size, size, axis)
            return own, other

        def reduce_scatter(own, other):
            total = (own.astype(F32) + flip_x(other).astype(F32)).astype(BF)
            r, cols = total.shape
            total = total.reshape((2,) * (bits - 1) + (r >> (bits - 1), cols))
            for n, bit in enumerate([1] + upper):
                axis = len(upper) if bit == 1 else 0
                keep = pick(total, rbit[bit], axis)
                send = pick(total, 1 - rbit[bit], axis)
                total = (keep.astype(F32) + flip(send, bit).astype(F32)).astype(BF)
            return total

        def gather(piece):
            for bit in [1] + upper[::-1] + [0]:
                other = flip(piece, bit)
                piece = ordered(rbit[bit], piece[None], other[None])
            return piece

        up_full = whole(up_own, up_pair)
        hidden = dot(normed_two, up_full) + up_bc
        cdf = 0.5 * (1.0 + lax.erf(hidden * (0.5**0.5)))
        active = (hidden * cdf).astype(BF)
        slope = cdf + hidden * jnp.exp(-0.5 * hidden * hidden) * ((2.0 * jnp.pi) ** -0.5)
        act_own, act_other = split(active, 1)
        down_other_grad = dot(act_other, cot, 0, 0, BF)
        down_own_grad = dot(act_own, cot, 0, 0, BF)
        down_piece = reduce_scatter(down_own_grad, down_other_grad)
        down_full = whole(down_own, down_pair)
        grad_hidden = (dot(cot, down_full, 1, 1) * slope).astype(BF)
        two_own, two_other = split(normed_two, 1)
        up_other_grad = dot(two_other, grad_hidden, 0, 0, BF)
        up_own_grad = dot(two_own, grad_hidden, 0, 0, BF)
        up_piece = reduce_scatter(up_own_grad, up_other_grad)
        grad_up_bias = jnp.sum(grad_hidden.astype(F32), axis=0)
        ffn_part = dot(active, down_full)
        grad_two = dot(grad_hidden, up_full, 1, 1)

        qkv_full = whole(qkv_own, qkv_pair)
        out_full = whole(out_own, out_pair)
        local = half // HD
        mixed = (dot(normed_one, qkv_full) + qkv_bc).reshape(2, length, 3, local, HD)
        documents = jnp.concatenate([segments, segments_other], 0)
        cosine, sine = jax.vmap(rotary_tables)(documents)
        queries = rotate(mixed[:, :, 0], cosine, sine).astype(BF)
        keys = rotate(mixed[:, :, 1], cosine, sine).astype(BF)
        values = mixed[:, :, 2].astype(BF)
        scale = HD**-0.5
        places = jnp.arange(length, dtype=jnp.int32)
        allowed = (documents[:, :, None] == documents[:, None, :]) & (
            places[None, None, :] <= places[None, :, None]
        )
        scores = jnp.einsum("sqhd,skhd->shqk", queries, keys, preferred_element_type=F32) * scale
        scores = jnp.where(allowed[:, None], scores, MASKED)
        weights = jnp.exp(scores - jnp.max(scores, axis=-1, keepdims=True))
        probs = weights / jnp.sum(weights, axis=-1, keepdims=True)
        probs_low = probs.astype(BF)
        context = jnp.einsum("shqk,skhd->sqhd", probs_low, values, preferred_element_type=F32)
        context = context.astype(BF).reshape(2 * length, half)
        attn_part = dot(context, out_full)
        grad_context = dot(cot, out_full, 1, 1).astype(BF).reshape(2, length, local, HD)
        grad_probs = jnp.einsum("sqhd,skhd->shqk", grad_context, values, preferred_element_type=F32)
        inner = jnp.sum(probs * grad_probs, axis=-1, keepdims=True)
        grad_scores = (probs * (grad_probs - inner)).astype(BF)
        grad_q = jnp.einsum("shqk,skhd->sqhd", grad_scores, keys, preferred_element_type=F32) * scale
        grad_k = jnp.einsum("shqk,sqhd->skhd", grad_scores, queries, preferred_element_type=F32) * scale
        grad_v = jnp.einsum("shqk,sqhd->skhd", probs_low, grad_context, preferred_element_type=F32)
        grad_q = rotate(grad_q, cosine, -sine)
        grad_k = rotate(grad_k, cosine, -sine)
        grad_mixed = jnp.stack([grad_q, grad_k, grad_v], axis=2).reshape(2 * length, 3 * half).astype(BF)
        one_own, one_other = split(normed_one, 1)
        qkv_other_grad = dot(one_other, grad_mixed, 0, 0, BF)
        qkv_own_grad = dot(one_own, grad_mixed, 0, 0, BF)
        qkv_piece = reduce_scatter(qkv_own_grad, qkv_other_grad)
        ctx_own, ctx_other = split(context, 1)

        def fold(array):
            return jnp.concatenate([array[:, :half], array[:, half:]], 0)

        out_piece = reduce_scatter(
            fold(dot(ctx_own, cot, 0, 0, BF)), fold(dot(ctx_other, cot, 0, 0, BF))
        )
        grad_one = dot(grad_mixed, qkv_full, 1, 1)

        def spread_core(vector, parts):
            size = vector.shape[0] // parts
            wide = jnp.stack([vector.reshape(parts, size)] * 2, axis=1)
            keep = (jnp.arange(2) == ci)[None, :, None]
            return jnp.where(keep, wide, 0.0).reshape(-1)

        column_sum = jnp.sum(cotangent.astype(F32), axis=0)
        small = jnp.concatenate(
            [
                jnp.sum(grad_one * unit, axis=0),
                jnp.sum(grad_one, axis=0),
                jnp.sum(grad_two * unit, axis=0),
                jnp.sum(grad_two, axis=0),
                column_sum,
                spread_core(jnp.sum(grad_mixed.astype(F32), axis=0), 6),
                spread_core(grad_up_bias, 2),
            ]
        ).reshape(-1, width)
        small = small + flip_x(small)
        for bit in range(bits):
            small = small + flip(small, bit)
        small = small.reshape(-1)

        part = attn_part + ffn_part
        output = (
            tokens.astype(F32)
            + (part[:length] + flip(part[length:], 0))
            + (out_b + down_b)
        ).astype(BF)
        pulled = grad_one * gain_one + grad_two * gain_two
        pulled = pulled[:length] + flip(pulled[length:], 0)
        unit_own = unit[:length]
        inward = spread[:length] * (
            pulled
            - jnp.mean(pulled, axis=-1, keepdims=True)
            - unit_own * jnp.mean(pulled * unit_own, axis=-1, keepdims=True)
        )
        grad_tokens = (cotangent.astype(F32) + inward).astype(BF)

        def rows_first(piece):
            return piece.reshape(2, -1, piece.shape[-1])

        down_all = rows_first(gather(down_piece)).reshape(ff_half, width).astype(F32)
        up_all = rows_first(gather(up_piece)).reshape(2, half, 2, ff_half // 2)
        up_all = jnp.transpose(up_all, (1, 2, 0, 3)).reshape(half, 2 * ff_half).astype(F32)
        qkv_all = rows_first(gather(qkv_piece)).reshape(2, half, 6, heads_core)
        qkv_all = jnp.transpose(qkv_all, (1, 2, 0, 3)).reshape(half, 6 * half).astype(F32)
        out_all = rows_first(gather(out_piece)).reshape(2, 2, heads_core, half)
        out_all = jnp.transpose(out_all, (0, 2, 1, 3)).reshape(half, width).astype(F32)

        def owned(start, size):
            return lax.dynamic_slice_in_dim(small, start + xi * size, size, 0)

        starts = [width * n for n in range(9)]
        bias_out = owned(starts[4], half)
        return (
            output,
            grad_tokens,
            owned(starts[0], half),
            owned(starts[1], half),
            owned(starts[2], half),
            owned(starts[3], half),
            qkv_all,
            owned(starts[5], 3 * half),
            out_all,
            bias_out,
            up_all,
            owned(starts[8], ff_half),
            down_all,
            bias_out,
        )

    return on_device


def solution(mesh):
    both = P(("rep", "shard"), None)
    vector = P("shard")
    matrix = P("shard", None)
    weights = (
        vector, vector, vector, vector, matrix, vector, matrix, vector, matrix, vector, matrix, vector,
    )
    return jax.shard_map(
        build(mesh.shape["rep"]),
        mesh=mesh,
        in_specs=(both, both) + weights + (both,),
        out_specs=(both, both) + weights,
        check_vma=False,
    )
```

time: 1200 us -> 681 us (0.57)
  blocking collectives: 562 us -> 0 us
  waiting for transfers between devices: 392 us -> 214 us
  local copies, waits for them, and re-layouts: 24.9 us -> 168 us
  other arithmetic: 44.8 us -> 116 us
  starting transfers between devices: 0.49 us -> 51.2 us
  matrix products: 142 us -> 118 us
  between operations: 17 us -> 2.55 us
    psum x1 -> x0, blocking collectives: 519 us -> none  [on_device(): lax.psum((owned[0], owned[1], owned[2], owned[3], owned[4], owned[5], own...]
    ppermute x0 -> x51, waiting for transfers between devices: none -> 214 us  [the longest x41 170 us: flip(): return lax.ppermute(array, 'rep', [(i, i ^ 1 << bit) for i in range(reps)])]
    reduce_scatter x4 -> x0, waiting for transfers between devices: 211 us -> none  [the longest x1 102 us: on_device(): lax.psum_scatter(grad_down.astype(jnp.bfloat16), 'shard', scatter_dimensi...]
    all_gather x4 -> x0, waiting for transfers between devices: 178 us -> none  [the longest x1 82.6 us: on_device(): lax.all_gather(down_weight, 'shard', axis=0, tiled=True)]
    ppermute x0 -> x51, starting transfers between devices: none -> 51.2 us  [the longest x41 38.6 us: flip(): return lax.ppermute(array, 'rep', [(i, i ^ 1 << bit) for i in range(reps)])]
    unnamed x97 -> x168, local copies, waits for them, and re-layouts: 11.6 us -> 56.7 us
    select_n x0 -> x32, other arithmetic: none -> 38 us  [ordered(): jnp.where(bit == 0, jnp.concatenate([own, other], axis), jnp.concatenate(...]
    all_gather x8 -> x0, blocking collectives: 35.6 us -> none  [the longest x1 5.25 us: on_device(): lax.all_gather(qkv_bias, 'shard', axis=0, tiled=True)]
  transfers between devices with their start and end apart: 8 -> 51, of which waited for: 6 -> 22; matrix products, arithmetic and copies ran while one was open for 17% -> 56% of each run, Pallas kernels for 0% -> 0%
where the time goes in v1:
time: 681 us; the launch traced here: 670 us
  waiting for transfers between devices  214 us (31%)
  local copies, waits for them, and re-layouts  168 us (25%)
  matrix products  118 us (17%)
  other arithmetic  116 us (17%)
  starting transfers between devices  51.2 us (8%)
    ppermute x41, waiting for transfers between devices, flip(): return lax.ppermute(array, 'rep', [(i, i ^ 1 << bit) for i in range(reps)])  170 us
    dot_general x16, matrix products, dot(): lax.dot_general(left, right, (((left_dim,), (right_dim,)), ((), ())), pre...  79.4 us
    unnamed x168, local copies, waits for them, and re-layouts  56.7 us
    ppermute x10, waiting for transfers between devices, flip_x(): return lax.ppermute(array, 'shard', [(0, 1), (1, 0)])  44.1 us
    ppermute x41, starting transfers between devices, flip(): return lax.ppermute(array, 'rep', [(i, i ^ 1 << bit) for i in range(reps)])  38.6 us
    select_n x32, other arithmetic, ordered(): jnp.where(bit == 0, jnp.concatenate([own, other], axis), jnp.concatenate(...  38 us
    convert_element_type x1, other arithmetic, on_device(): jnp.transpose(up_all, (1, 2, 0, 3)).reshape(half, 2 * ff_half).astype(F32)  20.6 us
    concatenate x5, local copies, waits for them, and re-layouts, ordered(): jnp.concatenate([own, other], axis)  16.6 us
  transfers between devices with their start and end apart: 51, of which 22 were waited for; matrix products, arithmetic and copies ran while one was open for 56% of the time, Pallas kernels for 0%

profile of v1, /device:TPU:0, one launch (start us, length us, event | category | flops | bytes accessed | tf_op | source)
XLA Modules:
  0.0 670.2 jit_solution(14696295857415818173)
XLA Ops:
  28.0 6.4 copy.83
  78.7 20.0 %collective-permute-done.9 = bf16[512,1024]{1,0:T(8,128)(2,1)} collective-permute-done((bf16[512,1024]{1,0:T(8,128)(2,1)}, bf16[512,1024]{1,0:T(8,128)(2,1)}, u32[]{:S(2)}, u32[]{:S(2)}) %collective-permute-start.9) | collective-permute-done | bytes 1048608 | tf_op jit(solution)/shard_map/ppermute | solution.py:50
  107.7 5.4 convolution_add_fusion
  113.1 10.3 %reshape.1453 = f32[2,512,3,8,64]{4,3,2,1,0:T(8,128)} reshape(f32[1024,1536]{1,0:T(8,128)} %convolution_add_fusion) | data formatting | bytes 12582912 | tf_op jit(solution)/shard_map/reshape | solution.py:168
  125.9 7.4 %fusion.112 = (f32[2,512,1,8,64]{4,3,2,1,0:T(8,128)}, f32[2,512,1,8,64]{4,3,2,1,0:T(8,128)}) fusion(f32[2,512,3,8,64]{4,3,2,1,0:T(8,128)} %reshape.1453), kind=kLoop, calls=%fused_computation.267 | loop fusion | bytes 8388608 | tf_op jit(solution)/shard_map/slice | solution.py:171
  152.4 11.4 %fusion.118 = (f32[2,8,512]{2,1,0:T(8,128)}, f32[2,8,512,512]{2,3,1,0:T(8,128)}) fusion(pred[2,512,512]{1,2,0:T(8,128)(4,1)} %compare_and_fusion, bf16[2,512,8,48]{1,3,2,0:T(8,128)(2,1)S(1)} %slice.274, bf16[2,512,8,16]{1,3,2,0:T(8,128)(2,1)S(1)} %get-tuple-element.63, bf16[2,512,8,48]{1,3,2,0:T(8,128)(2,1)} %slice.275, ...), kind=kOutput, calls=%fused_computation.273 | convolution fusion | flops 557842944 | bytes 19431424 | tf_op jit(solution)/shard_map/sub | solution.py:181
  163.8 8.7 %fusion.37 = bf16[2,512,8,64]{1,3,2,0:T(8,128)(2,1)} fusion(bf16[2,512,1,8,64]{1,4,3,0,2:T(8,128)(2,1)} %copy.113, f32[2,8,512,512]{2,3,1,0:T(8,128)} %get-tuple-element.87, f32[2,8,512]{2,1,0:T(8,128)} %get-tuple-element.86), kind=kOutput, calls=%fused_computation.93 | convolution fusion | flops 545783808 | bytes 18907136 | tf_op jit(solution)/shard_map/shqk,skhd->sqhd/dot_general | solution.py:184
  180.0 9.5 %multiply_reduce_fusion = (f32[2,8,512]{2,1,0:T(8,128)}, f32[2,8,512,512]{2,3,1,0:T(8,128)}) fusion(f32[2,8,512,512]{2,3,1,0:T(8,128)S(1)} %copy-done.2, f32[2,8,512]{2,1,0:T(8,128)} %get-tuple-element.86, bf16[2,512,8,64]{1,3,2,0:T(8,128)(2,1)} %copy.85, bf16[2,512,1,8,64]{1,4,3,0,2:T(8,128)(2,1)} %copy.113), kind=kOutput, calls=%fused_computation.2 | convolution fusion | flops 549445632 | bytes 35717120 | tf_op jit(solution)/shard_map/sqhd,skhd->shqk/dot_general | solution.py:188
  189.5 12.0 %multiply_convert_fusion = bf16[2,8,512,512]{2,3,1,0:T(8,128)(2,1)S(1)} fusion(f32[2,8,512,512]{2,3,1,0:T(8,128)} %get-tuple-element.89, f32[2,8,512]{2,1,0:T(8,128)} %get-tuple-element.88, f32[2,8,512,512]{2,3,1,0:T(8,128)} %get-tuple-element.87, f32[2,8,512]{2,1,0:T(8,128)} %get-tuple-element.86), kind=kLoop, calls=%fused_computation.1 | loop fusion | flops 16777216 | bytes 42008576 | tf_op jit(solution)/shard_map/convert_element_type | solution.py:190
  229.9 5.3 fusion.55
  238.7 8.1 %multiply_convert_fusion.1 = (bf16[1024,2048]{1,0:T(8,128)(2,1)S(1)}, f32[1024,2048]{1,0:T(8,128)}) fusion(f32[2048]{0:T(1024)S(1)} %bitcast.299, bf16[1024,1024]{1,0:T(8,128)(2,1)S(1)} %copy-done.12, bf16[512,2048]{0,1:T(8,128)(2,1)S(1)} %maximum_select_fusion.5, bf16[512,2048]{0,1:T(8,128)(2,1)S(1)} %bitcast.248, pred[]{:T(512)S(6)} %eq.28), kind=kOutput, calls=%fused_computation.16 | convolution fusion | flops 4326424576 | bytes 18882560 | tf_op jit(solution)/shard_map/dot_general | solution.py:17
  259.0 11.8 %convert_reduce_fusion = (f32[2048]{0:T(1024)S(1)}, bf16[1024,2048]{1,0:T(8,128)(2,1)S(1)}) fusion(f32[1024,2048]{1,0:T(8,128)} %get-tuple-element.93, f32[2048]{0:T(1024)S(1)} %bitcast.300, bf16[1024,1024]{1,0:T(8,128)(2,1)} %constant_dynamic-update-slice_fusion, bf16[1024,1024]{1,0:T(8,128)(2,1)S(1)} %maximum_select_fusion.6, ...), kind=kOutput, calls=%fused_computation.15 | convolution fusion | flops 4341102592 | bytes 18890752 | tf_op jit(solution)/shard_map/dot_general | solution.py:17
  270.8 11.5 %fusion.110 = (f32[1024]{0:T(1024)S(1)}, f32[1024]{0:T(1024)S(1)}, f32[1024,1024]{1,0:T(8,128)S(1)}, f32[1024]{0:T(1024)S(1)}, f32[1024]{0:T(1024)S(1)}, /*index=5*/f32[1024,1024]{1,0:T(8,128)}) fusion(f32[1024]{0:T(1024)S(1)} %copy-done.57, f32[1024]{0:T(1024)S(1)} %copy-done.55, bf16[512,1024]{1,0:T(8,128)(2,1)S(1)} %copy-done.6, ...), kind=kOutput, calls=%fused_computation.265 | convolution fusion | flops 4329566208 | bytes 23101440 | tf_op jit(solution)/shard_map/dot_general | solution.py:17
  320.0 5.6 collective-permute-done.33
  339.5 9.7 %collective-permute-done.20 = bf16[2,2,64,1536]{3,2,1,0:T(8,128)(2,1)S(1)} collective-permute-done((bf16[2,2,64,1536]{3,2,1,0:T(8,128)(2,1)S(1)}, bf16[2,2,64,1536]{3,2,1,0:T(8,128)(2,1)S(1)}, u32[]{:S(2)}, u32[]{:S(2)}) %collective-permute-start.20) | collective-permute-done | bytes 786464 | tf_op jit(solution)/shard_map/ppermute | solution.py:47
  358.5 5.3 add_convert_fusion.1
  363.8 19.9 %collective-permute-done.14 = f32[12,1024]{1,0:T(8,128)S(1)} collective-permute-done((f32[12,1024]{1,0:T(8,128)}, f32[12,1024]{1,0:T(8,128)S(1)}, u32[]{:S(2)}, u32[]{:S(2)}) %collective-permute-start.14) | collective-permute-done | bytes 49184 | tf_op jit(solution)/shard_map/ppermute | solution.py:50
  392.0 20.1 %collective-permute-done.16 = f32[12,1024]{1,0:T(8,128)S(1)} collective-permute-done((f32[12,1024]{1,0:T(8,128)S(1)}, f32[12,1024]{1,0:T(8,128)S(1)}, u32[]{:S(2)}, u32[]{:S(2)}) %collective-permute-start.16) | collective-permute-done | bytes 49184 | tf_op jit(solution)/shard_map/ppermute | solution.py:47
  425.5 17.3 %collective-permute-done.23 = bf16[64,1536]{1,0:T(8,128)(2,1)S(1)} collective-permute-done((bf16[64,1536]{1,0:T(8,128)(2,1)S(1)}, bf16[64,1536]{1,0:T(8,128)(2,1)S(1)}, u32[]{:S(2)}, u32[]{:S(2)}) %collective-permute-start.23) | collective-permute-done | bytes 196640 | tf_op jit(solution)/shard_map/ppermute | solution.py:47
  448.6 14.1 %collective-permute-done.24 = bf16[2,64,1536]{2,1,0:T(8,128)(2,1)S(1)} collective-permute-done((bf16[2,64,1536]{2,1,0:T(8,128)(2,1)S(1)}, bf16[2,64,1536]{2,1,0:T(8,128)(2,1)S(1)}, u32[]{:S(2)}, u32[]{:S(2)}) %collective-permute-start.24) | collective-permute-done | bytes 393248 | tf_op jit(solution)/shard_map/ppermute | solution.py:47
  463.1 11.1 %collective-permute-done.37 = bf16[2,64,2048]{2,1,0:T(8,128)(2,1)S(1)} collective-permute-done((bf16[2,64,2048]{2,1,0:T(8,128)(2,1)S(1)}, bf16[2,64,2048]{2,1,0:T(8,128)(2,1)S(1)}, u32[]{:S(2)}, u32[]{:S(2)}) %collective-permute-start.37) | collective-permute-done | bytes 524320 | tf_op jit(solution)/shard_map/ppermute | solution.py:47
  476.2 12.4 %collective-permute-done.38 = bf16[64,2048]{1,0:T(8,128)(2,1)S(1)} collective-permute-done((bf16[64,2048]{1,0:T(8,128)(2,1)S(1)}, bf16[64,2048]{1,0:T(8,128)(2,1)S(1)}, u32[]{:S(2)}, u32[]{:S(2)}) %collective-permute-start.38) | collective-permute-done | bytes 262176 | tf_op jit(solution)/shard_map/ppermute | solution.py:47
  490.4 11.9 %collective-permute-done.45 = bf16[2,128,1024]{2,1,0:T(8,128)(2,1)S(1)} collective-permute-done((bf16[2,128,1024]{2,1,0:T(8,128)(2,1)S(1)}, bf16[2,128,1024]{2,1,0:T(8,128)(2,1)S(1)}, u32[]{:S(2)}, u32[]{:S(2)}) %collective-permute-start.45) | collective-permute-done | bytes 524320 | tf_op jit(solution)/shard_map/ppermute | solution.py:47
  507.1 23.9 %collective-permute-done.40 = bf16[2,64,2048]{2,1,0:T(8,128)(2,1)S(1)} collective-permute-done((bf16[2,64,2048]{2,1,0:T(8,128)(2,1)S(1)}, bf16[2,64,2048]{2,1,0:T(8,128)(2,1)S(1)}, u32[]{:S(2)}, u32[]{:S(2)}) %collective-permute-start.40) | collective-permute-done | bytes 524320 | tf_op jit(solution)/shard_map/ppermute | solution.py:47
  547.6 20.2 %collective-permute-done.41 = bf16[2,2,64,2048]{3,2,1,0:T(8,128)(2,1)} collective-permute-done((bf16[2,2,64,2048]{3,2,1,0:T(8,128)(2,1)}, bf16[2,2,64,2048]{3,2,1,0:T(8,128)(2,1)}, u32[]{:S(2)}, u32[]{:S(2)}) %collective-permute-start.41) | collective-permute-done | bytes 1048608 | tf_op jit(solution)/shard_map/ppermute | solution.py:47
  581.2 6.4 convert_bitcast_fusion.1
  587.6 9.0 %copy.92 = f32[512,6,2,256]{0,3,2,1:T(8,128)} copy(f32[512,6,2,256]{3,1,0,2:T(8,128)} %convert_bitcast_fusion.1) | data formatting | bytes 12582912 | tf_op jit(solution)/shard_map/convert_element_type | solution.py:257
  596.6 6.6 copy.103
  608.7 7.6 %select_n.693 = bf16[1,512,2,1024]{3,0,2,1:T(2,128)(2,1)} reshape(bf16[1,2,2,2,64,2048]{5,4,3,2,1,0:T(8,128)(2,1)S(1)} %maximum_select_fusion.7) | data formatting | bytes 4194304 | tf_op jit(solution)/shard_map/jit(_where)/select_n | solution.py:65
  618.2 11.0 %concatenate.797 = bf16[1,512,2,1024]{3,0,2,1:T(2,128)(2,1)} reshape(bf16[2,2,2,64,2048]{4,3,2,1,0:T(8,128)(2,1)} %collective-permute-done.42) | data formatting | bytes 4194304 | tf_op jit(solution)/shard_map/concatenate | solution.py:67
  629.2 20.6 %convert_bitcast_fusion = f32[512,2,2,1024]{3,2,1,0:T(2,128)} fusion(pred[]{:T(512)S(6)} %eq.35, bf16[1,512,2,1024]{3,0,2,1:T(2,128)(2,1)} %concatenate.797, bf16[1,512,2,1024]{3,0,2,1:T(2,128)(2,1)} %select_n.693), kind=kLoop, calls=%fused_computation.13 | loop fusion | flops 20971520 | bytes 12582913 | tf_op jit(solution)/shard_map/convert_element_type | solution.py:255
  649.9 11.8 %reshape.1448 = f32[512,4096]{1,0:T(8,128)} reshape(f32[512,2,2,1024]{3,2,1,0:T(2,128)} %convert_bitcast_fusion) | data formatting | bytes 16777216 | tf_op jit(solution)/shard_map/convert_element_type | solution.py:255
  (428 shorter events, 295.4 us)
Async XLA Ops:
  12.3 36.8 %collective-permute-start.1 = (bf16[6656]{0:T(1024)(128)(2,1)}, bf16[6656]{0:T(1024)(128)(2,1)S(1)}, u32[]{:S(2)}, u32[]{:S(2)}) collective-permute-start(bf16[6656]{0:T(1024)(128)(2,1)} %dynamic-update-slice.16), channel_id=1, source_target_pairs={{0,1},{1,0},{2,3},{3,2},{4,5},{5,4},{6,7},{7,6},{8,9},{9,8},{10,11... | collective-permute-start | bytes 39944 | tf_op jit(solution)/shard_map/ppermute | solution.py:50
  15.3 61.1 %collective-permute-start = (bf16[512,1024]{1,0:T(8,128)(2,1)}, bf16[512,1024]{1,0:T(8,128)(2,1)S(1)}, u32[]{:S(2)}, u32[]{:S(2)}) collective-permute-start(bf16[512,1024]{1,0:T(8,128)(2,1)} %param.15), channel_id=1, source_target_pairs={{0,2},{2,0},{4,6},{6,4},{8,10},{10,8},{12,14},{14,12},{16,18},{18,... | collective-permute-start | bytes 3145736 | tf_op jit(solution)/shard_map/ppermute | solution.py:47
  24.8 39.4 %collective-permute-start.2 = (bf16[256,1536]{0,1:T(8,128)(2,1)}, bf16[256,1536]{0,1:T(8,128)(2,1)}, u32[]{:S(2)}, u32[]{:S(2)}) collective-permute-start(bf16[256,1536]{0,1:T(8,128)(2,1)} %constant_dynamic-slice_fusion.3), channel_id=1, source_target_pairs={{0,1},{1,0},{2,3},{3,2},{4,5},{5,4},{6,7},{7,6},{8,9},{9,8},{10,11... | collective-permute-start | bytes 2359304 | tf_op jit(solution)/shard_map/ppermute | solution.py:50
  25.3 40.5 %collective-permute-start.12 = (bf16[512,1024]{1,0:T(8,128)(2,1)S(1)}, bf16[512,1024]{1,0:T(8,128)(2,1)}, u32[]{:S(2)}, u32[]{:S(2)}) collective-permute-start(bf16[512,1024]{1,0:T(8,128)(2,1)S(1)} %copy-done.19), channel_id=1, source_target_pairs={{0,2},{2,0},{4,6},{6,4},{8,10},{10,8},{12,14},{14,12},{16,18},{18,... | collective-permute-start | bytes 3145736 | tf_op jit(solution)/shard_map/ppermute | solution.py:47
  49.1 28.4 %collective-permute-start.7 = (bf16[256,2048]{0,1:T(8,128)(2,1)}, bf16[256,2048]{0,1:T(8,128)(2,1)}, u32[]{:S(2)}, u32[]{:S(2)}) collective-permute-start(bf16[256,2048]{0,1:T(8,128)(2,1)} %constant_dynamic-slice_fusion), channel_id=1, source_target_pairs={{0,1},{1,0},{2,3},{3,2},{4,5},{5,4},{6,7},{7,6},{8,9},{9,8},{10,11... | collective-permute-start | bytes 3145736 | tf_op jit(solution)/shard_map/ppermute | solution.py:50
  61.5 37.2 %collective-permute-start.9 = (bf16[512,1024]{1,0:T(8,128)(2,1)}, bf16[512,1024]{1,0:T(8,128)(2,1)}, u32[]{:S(2)}, u32[]{:S(2)}) collective-permute-start(bf16[512,1024]{1,0:T(8,128)(2,1)} %dynamic-slice_bitcast_fusion.3), channel_id=1, source_target_pairs={{0,1},{1,0},{2,3},{3,2},{4,5},{5,4},{6,7},{7,6},{8,9},{9,8},{10,11... | collective-permute-start | bytes 3145736 | tf_op jit(solution)/shard_map/ppermute | solution.py:50
  64.3 39.3 %collective-permute-start.3 = (bf16[256,1536]{0,1:T(8,128)(2,1)}, bf16[256,1536]{0,1:T(8,128)(2,1)}, u32[]{:S(2)}, u32[]{:S(2)}) collective-permute-start(bf16[256,1536]{0,1:T(8,128)(2,1)} %collective-permute-done.2), channel_id=1, source_target_pairs={{0,4},{2,6},{4,0},{6,2},{8,12},{10,14},{12,8},{14,10},{16,20},{18,... | collective-permute-start | bytes 2359304 | tf_op jit(solution)/shard_map/ppermute | solution.py:47
  77.5 157.7 %collective-permute-start.8 = (bf16[256,2048]{0,1:T(8,128)(2,1)}, bf16[256,2048]{0,1:T(8,128)(2,1)}, u32[]{:S(2)}, u32[]{:S(2)}) collective-permute-start(bf16[256,2048]{0,1:T(8,128)(2,1)} %collective-permute-done.7), channel_id=1, source_target_pairs={{0,4},{2,6},{4,0},{6,2},{8,12},{10,14},{12,8},{14,10},{16,20},{18,... | collective-permute-start | bytes 3145736 | tf_op jit(solution)/shard_map/ppermute | solution.py:47
  98.7 148.1 %collective-permute-start.10 = (bf16[512,1024]{1,0:T(8,128)(2,1)}, bf16[512,1024]{1,0:T(8,128)(2,1)}, u32[]{:S(2)}, u32[]{:S(2)}) collective-permute-start(bf16[512,1024]{1,0:T(8,128)(2,1)} %collective-permute-done.9), channel_id=1, source_target_pairs={{0,4},{2,6},{4,0},{6,2},{8,12},{10,14},{12,8},{14,10},{16,20},{18,... | collective-permute-start | bytes 3145736 | tf_op jit(solution)/shard_map/ppermute | solution.py:47
  224.6 101.2 %collective-permute-start.19 = (bf16[512,1536]{1,0:T(8,128)(2,1)}, bf16[512,1536]{1,0:T(8,128)(2,1)}, u32[]{:S(2)}, u32[]{:S(2)}) collective-permute-start(bf16[512,1536]{1,0:T(8,128)(2,1)} %fusion.49), channel_id=1, source_target_pairs={{0,1},{1,0},{2,3},{3,2},{4,5},{5,4},{6,7},{7,6},{8,9},{9,8},{10,11... | collective-permute-start | bytes 4718600 | tf_op jit(solution)/shard_map/ppermute | solution.py:50
  227.7 58.7 %collective-permute-start.27 = (bf16[512,512]{1,0:T(8,128)(2,1)}, bf16[512,512]{1,0:T(8,128)(2,1)}, u32[]{:S(2)}, u32[]{:S(2)}) collective-permute-start(bf16[512,512]{1,0:T(8,128)(2,1)} %pad_maximum_fusion.3), channel_id=1, source_target_pairs={{0,1},{1,0},{2,3},{3,2},{4,5},{5,4},{6,7},{7,6},{8,9},{9,8},{10,11... | collective-permute-start | bytes 1572872 | tf_op jit(solution)/shard_map/ppermute | solution.py:50
  257.8 162.4 %collective-permute-start.11 = (f32[512,1024]{1,0:T(8,128)}, f32[512,1024]{1,0:T(8,128)}, u32[]{:S(2)}, u32[]{:S(2)}) collective-permute-start(f32[512,1024]{1,0:T(8,128)} %slice.216), channel_id=1, source_target_pairs={{0,2},{2,0},{4,6},{6,4},{8,10},{10,8},{12,14},{14,12},{16,18},{18,... | collective-permute-start | bytes 6291464 | tf_op jit(solution)/shard_map/ppermute | solution.py:47
  282.5 68.4 %collective-permute-start.13 = (f32[512,1024]{1,0:T(8,128)S(1)}, f32[512,1024]{1,0:T(8,128)S(1)}, u32[]{:S(2)}, u32[]{:S(2)}) collective-permute-start(f32[512,1024]{1,0:T(8,128)S(1)} %slice.230), channel_id=1, source_target_pairs={{0,2},{2,0},{4,6},{6,4},{8,10},{10,8},{12,14},{14,12},{16,18},{18,... | collective-permute-start | bytes 6291464 | tf_op jit(solution)/shard_map/ppermute | solution.py:47
  288.4 70.1 %collective-permute-start.35 = (bf16[512,2048]{1,0:T(8,128)(2,1)}, bf16[512,2048]{1,0:T(8,128)(2,1)}, u32[]{:S(2)}, u32[]{:S(2)}) collective-permute-start(bf16[512,2048]{1,0:T(8,128)(2,1)} %fusion.46), channel_id=1, source_target_pairs={{0,1},{1,0},{2,3},{3,2},{4,5},{5,4},{6,7},{7,6},{8,9},{9,8},{10,11... | collective-permute-start | bytes 6291464 | tf_op jit(solution)/shard_map/ppermute | solution.py:50
  334.3 55.1 %collective-permute-start.43 = (bf16[1024,1024]{1,0:T(8,128)(2,1)}, bf16[1024,1024]{1,0:T(8,128)(2,1)}, u32[]{:S(2)}, u32[]{:S(2)}) collective-permute-start(bf16[1024,1024]{1,0:T(8,128)(2,1)} %fusion.24), channel_id=1, source_target_pairs={{0,1},{1,0},{2,3},{3,2},{4,5},{5,4},{6,7},{7,6},{8,9},{9,8},{10,11... | collective-permute-start | bytes 6291464 | tf_op jit(solution)/shard_map/ppermute | solution.py:50
  350.3 36.8 %collective-permute-start.21 = (bf16[2,64,1536]{2,1,0:T(8,128)(2,1)}, bf16[2,64,1536]{2,1,0:T(8,128)(2,1)S(1)}, u32[]{:S(2)}, u32[]{:S(2)}) collective-permute-start(bf16[2,64,1536]{2,1,0:T(8,128)(2,1)} %dynamic-slice_bitcast_fusion.8), channel_id=1, source_target_pairs={{0,8},{2,10},{4,12},{6,14},{8,0},{10,2},{12,4},{14,6},{16,24},{18,... | collective-permute-start | bytes 1179656 | tf_op jit(solution)/shard_map/ppermute | solution.py:47
  357.1 26.6 %collective-permute-start.14 = (f32[12,1024]{1,0:T(8,128)}, f32[12,1024]{1,0:T(8,128)S(1)}, u32[]{:S(2)}, u32[]{:S(2)}) collective-permute-start(f32[12,1024]{1,0:T(8,128)} %reshape.1431), channel_id=1, source_target_pairs={{0,1},{1,0},{2,3},{3,2},{4,5},{5,4},{6,7},{7,6},{8,9},{9,8},{10,11... | collective-permute-start | bytes 147464 | tf_op jit(solution)/shard_map/ppermute | solution.py:50
  384.9 61.6 %collective-permute-start.36 = (bf16[2,2,64,2048]{3,2,1,0:T(8,128)(2,1)}, bf16[2,2,64,2048]{3,2,1,0:T(8,128)(2,1)}, u32[]{:S(2)}, u32[]{:S(2)}) collective-permute-start(bf16[2,2,64,2048]{3,2,1,0:T(8,128)(2,1)} %dynamic-slice_bitcast_fusion.2), channel_id=1, source_target_pairs={{0,4},{2,6},{4,0},{6,2},{8,12},{10,14},{12,8},{14,10},{16,20},{18,... | collective-permute-start | bytes 3145736 | tf_op jit(solution)/shard_map/ppermute | solution.py:47
  386.4 25.6 %collective-permute-start.16 = (f32[12,1024]{1,0:T(8,128)S(1)}, f32[12,1024]{1,0:T(8,128)S(1)}, u32[]{:S(2)}, u32[]{:S(2)}) collective-permute-start(f32[12,1024]{1,0:T(8,128)S(1)} %add.340), channel_id=1, source_target_pairs={{0,4},{2,6},{4,0},{6,2},{8,12},{10,14},{12,8},{14,10},{16,20},{18,... | collective-permute-start | bytes 147464 | tf_op jit(solution)/shard_map/ppermute | solution.py:47
  387.2 31.8 %collective-permute-start.22 = (bf16[64,1536]{1,0:T(8,128)(2,1)S(1)}, bf16[64,1536]{1,0:T(8,128)(2,1)S(1)}, u32[]{:S(2)}, u32[]{:S(2)}) collective-permute-start(bf16[64,1536]{1,0:T(8,128)(2,1)S(1)} %dynamic-slice_bitcast_fusion.13), channel_id=1, source_target_pairs={{0,16},{2,18},{4,20},{6,22},{8,24},{10,26},{12,28},{14,30},{16,0},... | collective-permute-start | bytes 589832 | tf_op jit(solution)/shard_map/ppermute | solution.py:47
  413.9 60.6 %collective-permute-start.44 = (bf16[2,2,128,1024]{3,2,1,0:T(8,128)(2,1)}, bf16[2,2,128,1024]{3,2,1,0:T(8,128)(2,1)}, u32[]{:S(2)}, u32[]{:S(2)}) collective-permute-start(bf16[2,2,128,1024]{3,2,1,0:T(8,128)(2,1)} %dynamic-slice_bitcast_fusion.1), channel_id=1, source_target_pairs={{0,4},{2,6},{4,0},{6,2},{8,12},{10,14},{12,8},{14,10},{16,20},{18,... | collective-permute-start | bytes 3145736 | tf_op jit(solution)/shard_map/ppermute | solution.py:47
  448.2 26.0 %collective-permute-start.37 = (bf16[2,64,2048]{2,1,0:T(8,128)(2,1)S(1)}, bf16[2,64,2048]{2,1,0:T(8,128)(2,1)S(1)}, u32[]{:S(2)}, u32[]{:S(2)}) collective-permute-start(bf16[2,64,2048]{2,1,0:T(8,128)(2,1)S(1)} %dynamic-slice_bitcast_fusion.6), channel_id=1, source_target_pairs={{0,8},{2,10},{4,12},{6,14},{8,0},{10,2},{12,4},{14,6},{16,24},{18,... | collective-permute-start | bytes 1572872 | tf_op jit(solution)/shard_map/ppermute | solution.py:47
  462.8 42.8 %collective-permute-start.25 = (bf16[2,2,64,1536]{3,2,1,0:T(8,128)(2,1)S(1)}, bf16[2,2,64,1536]{3,2,1,0:T(8,128)(2,1)S(1)}, u32[]{:S(2)}, u32[]{:S(2)}) collective-permute-start(bf16[2,2,64,1536]{3,2,1,0:T(8,128)(2,1)S(1)} %maximum_select_fusion.21), channel_id=1, source_target_pairs={{0,8},{2,10},{4,12},{6,14},{8,0},{10,2},{12,4},{14,6},{16,24},{18,... | collective-permute-start | bytes 2359304 | tf_op jit(solution)/shard_map/ppermute | solution.py:47
  476.1 26.2 %collective-permute-start.45 = (bf16[2,128,1024]{2,1,0:T(8,128)(2,1)S(1)}, bf16[2,128,1024]{2,1,0:T(8,128)(2,1)S(1)}, u32[]{:S(2)}, u32[]{:S(2)}) collective-permute-start(bf16[2,128,1024]{2,1,0:T(8,128)(2,1)S(1)} %dynamic-slice_bitcast_fusion.5), channel_id=1, source_target_pairs={{0,8},{2,10},{4,12},{6,14},{8,0},{10,2},{12,4},{14,6},{16,24},{18,... | collective-permute-start | bytes 1572872 | tf_op jit(solution)/shard_map/ppermute | solution.py:47
  502.6 28.5 %collective-permute-start.40 = (bf16[2,64,2048]{2,1,0:T(8,128)(2,1)S(1)}, bf16[2,64,2048]{2,1,0:T(8,128)(2,1)S(1)}, u32[]{:S(2)}, u32[]{:S(2)}) collective-permute-start(bf16[2,64,2048]{2,1,0:T(8,128)(2,1)S(1)} %maximum_select_fusion.32), channel_id=1, source_target_pairs={{0,16},{2,18},{4,20},{6,22},{8,24},{10,26},{12,28},{14,30},{16,0},... | collective-permute-start | bytes 1572872 | tf_op jit(solution)/shard_map/ppermute | solution.py:47
  502.7 34.0 %collective-permute-start.46 = (bf16[128,1024]{1,0:T(8,128)(2,1)S(1)}, bf16[128,1024]{1,0:T(8,128)(2,1)S(1)}, u32[]{:S(2)}, u32[]{:S(2)}) collective-permute-start(bf16[128,1024]{1,0:T(8,128)(2,1)S(1)} %dynamic-slice_bitcast_fusion.9), channel_id=1, source_target_pairs={{0,16},{2,18},{4,20},{6,22},{8,24},{10,26},{12,28},{14,30},{16,0},... | collective-permute-start | bytes 786440 | tf_op jit(solution)/shard_map/ppermute | solution.py:47
  507.1 69.9 %collective-permute-start.26 = (bf16[2,2,2,64,1536]{4,3,2,1,0:T(8,128)(2,1)}, bf16[2,2,2,64,1536]{4,3,2,1,0:T(8,128)(2,1)}, u32[]{:S(2)}, u32[]{:S(2)}) collective-permute-start(bf16[2,2,2,64,1536]{4,3,2,1,0:T(8,128)(2,1)} %maximum_select_fusion.13), channel_id=1, source_target_pairs={{0,2},{2,0},{4,6},{6,4},{8,10},{10,8},{12,14},{14,12},{16,18},{18,... | collective-permute-start | bytes 4718600 | tf_op jit(solution)/shard_map/ppermute | solution.py:47
  532.2 35.6 %collective-permute-start.41 = (bf16[2,2,64,2048]{3,2,1,0:T(8,128)(2,1)}, bf16[2,2,64,2048]{3,2,1,0:T(8,128)(2,1)}, u32[]{:S(2)}, u32[]{:S(2)}) collective-permute-start(bf16[2,2,64,2048]{3,2,1,0:T(8,128)(2,1)} %maximum_select_fusion.16), channel_id=1, source_target_pairs={{0,8},{2,10},{4,12},{6,14},{8,0},{10,2},{12,4},{14,6},{16,24},{18,... | collective-permute-start | bytes 3145736 | tf_op jit(solution)/shard_map/ppermute | solution.py:47
  546.2 25.1 %collective-permute-start.48 = (bf16[2,128,1024]{2,1,0:T(8,128)(2,1)S(1)}, bf16[2,128,1024]{2,1,0:T(8,128)(2,1)S(1)}, u32[]{:S(2)}, u32[]{:S(2)}) collective-permute-start(bf16[2,128,1024]{2,1,0:T(8,128)(2,1)S(1)} %maximum_select_fusion.34), channel_id=1, source_target_pairs={{0,16},{2,18},{4,20},{6,22},{8,24},{10,26},{12,28},{14,30},{16,0},... | collective-permute-start | bytes 1572872 | tf_op jit(solution)/shard_map/ppermute | solution.py:47
  571.0 47.2 %collective-permute-start.42 = (bf16[2,2,2,64,2048]{4,3,2,1,0:T(8,128)(2,1)}, bf16[2,2,2,64,2048]{4,3,2,1,0:T(8,128)(2,1)}, u32[]{:S(2)}, u32[]{:S(2)}) collective-permute-start(bf16[2,2,2,64,2048]{4,3,2,1,0:T(8,128)(2,1)} %maximum_select_fusion.8), channel_id=1, source_target_pairs={{0,2},{2,0},{4,6},{6,4},{8,10},{10,8},{12,14},{14,12},{16,18},{18,... | collective-permute-start | bytes 6291464 | tf_op jit(solution)/shard_map/ppermute | solution.py:47
  572.4 30.8 %collective-permute-start.49 = (bf16[2,2,128,1024]{3,2,1,0:T(8,128)(2,1)}, bf16[2,2,128,1024]{3,2,1,0:T(8,128)(2,1)}, u32[]{:S(2)}, u32[]{:S(2)}) collective-permute-start(bf16[2,2,128,1024]{3,2,1,0:T(8,128)(2,1)} %maximum_select_fusion.19), channel_id=1, source_target_pairs={{0,8},{2,10},{4,12},{6,14},{8,0},{10,2},{12,4},{14,6},{16,24},{18,... | collective-permute-start | bytes 3145736 | tf_op jit(solution)/shard_map/ppermute | solution.py:47
  606.5 55.1 %collective-permute-start.50 = (bf16[2,2,2,128,1024]{4,3,2,1,0:T(8,128)(2,1)}, bf16[2,2,2,128,1024]{4,3,2,1,0:T(8,128)(2,1)}, u32[]{:S(2)}, u32[]{:S(2)}) collective-permute-start(bf16[2,2,2,128,1024]{4,3,2,1,0:T(8,128)(2,1)} %maximum_select_fusion.10), channel_id=1, source_target_pairs={{0,2},{2,0},{4,6},{6,4},{8,10},{10,8},{12,14},{14,12},{16,18},{18,... | collective-permute-start | bytes 6291464 | tf_op jit(solution)/shard_map/ppermute | solution.py:47
  (91 other events, 1344.5 us)

commit v2 on v1

v2 whole, which is shorter than its diff:
```python
import jax
import jax.numpy as jnp
from jax import lax
from jax.experimental import pallas as pl
from jax.experimental.pallas import tpu as pltpu
from jax.sharding import PartitionSpec as P

HD = 64
ROT = 16
EPSILON = 1e-05
MASKED = -1e30
BF = jnp.bfloat16
F32 = jnp.float32
TILE = 512
MIB = 1 << 20
NN = (((1,), (0,)), ((), ()))
NT = (((1,), (1,)), ((), ()))
TN = (((0,), (0,)), ((), ()))


def mm(left, right, dims=NN):
    return lax.dot_general(left, right, dims, preferred_element_type=F32)


def cost(flops, nbytes):
    return pl.CostEstimate(flops=int(flops), bytes_accessed=int(nbytes), transcendentals=0)


def params(mib):
    return pltpu.CompilerParams(vmem_limit_bytes=mib * MIB)


ANY = pl.BlockSpec(memory_space=pl.ANY)


def held(shape):
    return pl.BlockSpec(shape, lambda *_: (0,) * len(shape), pipeline_mode=pl.Buffered(1))


def sds(shape, kind):
    return jax.ShapeDtypeStruct(shape, kind)


def copy_all(pairs, sems):
    copies = [pltpu.make_async_copy(a, b, sems.at[n]) for n, (a, b) in enumerate(pairs)]
    for c in copies:
        c.start()
    for c in copies:
        c.wait()


def place(index):
    return index[0], index[1], index[2], index[3]


def quarters(index):
    _, _, y, z = place(index)
    return (2 * y + z, 2 * (1 - y) + z, 2 * y + (1 - z), 2 * (1 - y) + (1 - z))


def pack_up_kernel(index, weight, out, sems):
    x, c, y, z = place(index)
    half = weight.shape[0]
    rows = half // 4
    wide = weight.shape[1] // 4
    row = pl.ds(pl.multiple_of((2 * y + z) * rows, rows), rows)
    copy_all(
        [
            (weight.at[row, pl.ds(pl.multiple_of((2 * h + c) * wide, wide), wide)], out.at[:, pl.ds(h * wide, wide)])
            for h in range(2)
        ],
        sems,
    )


def pack_rest_kernel(index, down, qkv, out_w, down_out, rest_out, sems):
    x, c, y, z = place(index)
    q = 2 * y + z
    rows = down.shape[0] // 8
    pairs = [(down.at[pl.ds(pl.multiple_of((4 * c + q) * rows, rows), rows)], down_out)]
    half = qkv.shape[0]
    rows = half // 4
    wide = half // 2
    for t in range(3):
        for h in range(2):
            col = pl.multiple_of((4 * t + 2 * h + c) * wide, wide)
            pairs.append(
                (
                    qkv.at[pl.ds(pl.multiple_of(q * rows, rows), rows), pl.ds(col, wide)],
                    rest_out.at[:, pl.ds((2 * t + h) * wide, wide)],
                )
            )
    rows = half // 8
    for h in range(2):
        pairs.append(
            (
                out_w.at[pl.ds(pl.multiple_of((4 * c + q) * rows, rows), rows), pl.ds(h * half, half)],
                rest_out.at[pl.ds(h * rows, rows), pl.ds(3 * half, half)],
            )
        )
    copy_all(pairs, sems)


def up_pairs(index, weight, pieces, dest, side):
    x, c, _, _ = place(index)
    half = weight.shape[0]
    rows = half // 4
    wide = weight.shape[1] // 4
    pairs = [
        (
            weight.at[:, pl.ds(pl.multiple_of((2 * side + c) * wide, wide), wide)],
            dest.at[pl.ds(pl.multiple_of(x * half, half), half)],
        )
    ]
    for q, piece in zip(quarters(index), pieces):
        pairs.append(
            (
                piece.at[:, pl.ds(pl.multiple_of(side * wide, wide), wide)],
                dest.at[pl.ds(pl.multiple_of((1 - x) * half + q * rows, rows), rows)],
            )
        )
    return pairs


BLOCK = 256


def gelu_parts(hidden):
    cdf = 0.5 * (1.0 + lax.erf(hidden * (0.5**0.5)))
    slope = cdf + hidden * jnp.exp(-0.5 * hidden * hidden) * ((2.0 * jnp.pi) ** -0.5)
    return (hidden * cdf).astype(BF), slope


def ffn_other_kernel(index, normed, cot, bias, weight, p0, p1, p2, p3, act, slope, grad, w_all, sems):
    x = index[0]
    j = pl.program_id(0)

    @pl.when(j == 0)
    def _():
        copy_all(up_pairs(index, weight, (p0, p1, p2, p3), w_all, 1 - x), sems)

    w = w_all[:, pl.ds(pl.multiple_of(j * BLOCK, BLOCK), BLOCK)]
    hidden = mm(normed[...], w) + bias[...]
    a, s = gelu_parts(hidden)
    act[...] = a
    slope[...] = s.astype(BF)
    g = mm(a, cot[...], TN).astype(BF)
    grad[0] = g[:, :TILE]
    grad[1] = g[:, TILE:]


def ffn_own_kernel(
    index, normed, cot, bias, down, weight, p0, p1, p2, p3,
    act, hid, grad_down, up_send, up_keep, colsum, w_all, sems,
):
    x = index[0]
    j = pl.program_id(0)

    @pl.when(j == 0)
    def _():
        copy_all(up_pairs(index, weight, (p0, p1, p2, p3), w_all, x), sems)

    w = w_all[:, pl.ds(pl.multiple_of(j * BLOCK, BLOCK), BLOCK)]
    hidden = mm(normed[...], w) + bias[...]
    a, s = gelu_parts(hidden)
    act[...] = a
    g = mm(a, cot[...], TN).astype(BF)
    grad_down[0] = g[:, :TILE]
    grad_down[1] = g[:, TILE:]
    gh = mm(cot[...], down[...], NT) * s
    low = gh.astype(BF)
    hid[...] = low
    colsum[...] = jnp.sum(low.astype(F32), axis=0, keepdims=True)
    up_send[0] = mm(normed[:, pl.ds(pl.multiple_of((1 - x) * TILE, TILE), TILE)], low, TN).astype(BF)
    up_keep[0] = mm(normed[:, pl.ds(pl.multiple_of(x * TILE, TILE), TILE)], low, TN).astype(BF)


def ffn_back_kernel(index, normed, cot, slope, d0, d1, d2, d3, hid, up_send, up_keep, colsum, d_all, sems):
    x = index[0]
    j = pl.program_id(0)
    rows = d0.shape[0]

    @pl.when(j == 0)
    def _():
        copy_all(
            [
                (piece, d_all.at[pl.ds(pl.multiple_of(q * rows, rows), rows)])
                for q, piece in zip(quarters(index), (d0, d1, d2, d3))
            ],
            sems,
        )

    d = d_all[pl.ds(pl.multiple_of(j * BLOCK, BLOCK), BLOCK), :]
    low = (mm(cot[...], d, NT) * slope[...].astype(F32)).astype(BF)
    hid[...] = low
    colsum[...] = jnp.sum(low.astype(F32), axis=0, keepdims=True)
    up_send[0] = mm(normed[:, pl.ds(pl.multiple_of((1 - x) * TILE, TILE), TILE)], low, TN).astype(BF)
    up_keep[0] = mm(normed[:, pl.ds(pl.multiple_of(x * TILE, TILE), TILE)], low, TN).astype(BF)


def ffn_last_kernel(
    index, act_o, act_x, hid_o, hid_x, down, d0, d1, d2, d3, weight, p0, p1, p2, p3,
    out, grad, w_o, w_x, d_o, d_x, sems,
):
    x, c, _, _ = place(index)

    @pl.when(pl.program_id(0) == 0)
    def _():
        rows = d0.shape[0]
        wide = d_o.shape[0]
        pairs = up_pairs(index, weight, (p0, p1, p2, p3), w_o, x)
        pairs += up_pairs(index, weight, (p0, p1, p2, p3), w_x, 1 - x)
        pairs.append((down.at[pl.ds(pl.multiple_of(c * wide, wide), wide)], d_o))
        for q, piece in zip(quarters(index), (d0, d1, d2, d3)):
            pairs.append((piece, d_x.at[pl.ds(pl.multiple_of(q * rows, rows), rows)]))
        copy_all(pairs, sems)

    out[...] = mm(act_o[...], d_o[...]) + mm(act_x[...], d_x[...])
    grad[...] = mm(hid_o[...], w_o[...], NT) + mm(hid_x[...], w_x[...], NT)


def attention_kernel(
    index, normed, cot, cosine, sine_low, sine_high, doc_col, doc_row, bias, qkv, out_w, p0, p1, p2, p3,
    send, keep, grad_normed, result, colsum, w_all, o_all, mask, sems,
):
    x, c, _, _ = place(index)
    p = pl.program_id(0)
    half = qkv.shape[0]
    quarter = half // 4
    pair = 2 * HD
    length = doc_row.shape[1]

    @pl.when(p == 0)
    def _():
        pairs = []
        own = pl.ds(pl.multiple_of(x * half, half), half)
        wide = half // 2
        for t in range(3):
            for h in range(2):
                col = pl.multiple_of((4 * t + 2 * h + c) * wide, wide)
                pairs.append((qkv.at[:, pl.ds(col, wide)], w_all.at[own, pl.ds((2 * t + h) * wide, wide)]))
        pairs.append(
            (
                out_w.at[pl.ds(pl.multiple_of(c * wide, wide), wide)],
                o_all.at[pl.ds(pl.multiple_of(x * wide, wide), wide)],
            )
        )
        eighth = half // 8
        for q, piece in zip(quarters(index), (p0, p1, p2, p3)):
            row = pl.multiple_of((1 - x) * half + q * quarter, quarter)
            pairs.append((piece.at[:, pl.ds(0, 3 * half)], w_all.at[pl.ds(row, quarter)]))
            row = pl.multiple_of((1 - x) * wide + q * eighth, eighth)
            for h in range(2):
                pairs.append(
                    (
                        piece.at[pl.ds(h * eighth, eighth), pl.ds(3 * half, half)],
                        o_all.at[pl.ds(row, eighth), pl.ds(h * half, half)],
                    )
                )
        copies = [pltpu.make_async_copy(a, b, sems.at[n]) for n, (a, b) in enumerate(pairs)]
        for copy in copies:
            copy.start()
        for s in range(2):
            keys = lax.broadcasted_iota(jnp.int32, (length, length), 0)
            queries = lax.broadcasted_iota(jnp.int32, (length, length), 1)
            same = doc_col[s * length : (s + 1) * length, :] == doc_row[s : s + 1, :]
            mask[s] = jnp.where(same & (keys <= queries), 0.0, MASKED)
        for copy in copies:
            copy.wait()

    def lanes(t):
        return pl.ds(pl.multiple_of(t * half + p * pair, pair), pair)

    w = jnp.concatenate([w_all[:, lanes(t)] for t in range(3)], axis=1)
    wo = o_all[pl.ds(pl.multiple_of(p * pair, pair), pair), :]
    b = jnp.concatenate([bias[:, lanes(t)] for t in range(3)], axis=1)
    mixed = mm(normed[...], w) + b
    cs, lo, hi = cosine[...], sine_low[...], sine_high[...]

    def turn(v, sign):
        return v * cs + sign * (pltpu.roll(v, pair - ROT // 2, 1) * lo + pltpu.roll(v, ROT // 2, 1) * hi)

    scale = HD**-0.5
    q_all = turn(mixed[:, :pair], 1.0).astype(BF)
    k_all = turn(mixed[:, pair : 2 * pair], 1.0).astype(BF)
    v_f32 = mixed[:, 2 * pair :].astype(BF).astype(F32)
    v_all = v_f32.astype(BF)
    q_all = (q_all.astype(F32) * scale).astype(BF)
    gc_all = mm(cot[...], wo, NT).astype(BF)
    lane = lax.broadcasted_iota(jnp.int32, (length, pair), 1)
    first = lane < HD
    zero = jnp.zeros((length, pair), BF)
    part = length // 2
    contexts, mixed_grads = [], []
    for s in range(2):
        row = slice(s * length, (s + 1) * length)
        q, k, v, gc = q_all[row], k_all[row], v_all[row], gc_all[row]
        k_turned = k.astype(F32).T.astype(BF)
        v_turned = v_f32[row].T.astype(BF)
        context_t, query_t, grad_k, grad_v = [], [], [], []
        for h in range(2):
            mine = first if h == 0 else ~first
            qm = jnp.where(mine, q, zero)
            gm = jnp.where(mine, gc, zero)
            rows_h = slice(h * HD, (h + 1) * HD)
            ct, qt = [], []
            dk = dv = None
            for block in range(2):
                kk = part * (block + 1)
                qs = slice(block * part, (block + 1) * part)
                scores = mm(k[:kk], qm[qs], NT) + mask[s, :kk, qs]
                weights = jnp.exp(scores - jnp.max(scores, axis=0, keepdims=True))
                probs = weights * (1.0 / jnp.sum(weights, axis=0, keepdims=True))
                low = probs.astype(BF)
                ct.append(mm(v_turned[rows_h, :kk], low))
                grad_probs = mm(v[:kk], gm[qs], NT)
                inner = jnp.sum(probs * grad_probs, axis=0, keepdims=True)
                ds = (probs * (grad_probs - inner)).astype(BF)
                qt.append(mm(k_turned[rows_h, :kk], ds))
                dv_b = mm(low, gc[qs])
                dk_b = mm(ds, q[qs])
                if block == 0:
                    dv, dk = dv_b, dk_b
                else:
                    dv = jnp.concatenate([dv + dv_b[:part], dv_b[part:]], axis=0)
                    dk = jnp.concatenate([dk + dk_b[:part], dk_b[part:]], axis=0)
            context_t.append(jnp.concatenate(ct, axis=1))
            query_t.append(jnp.concatenate(qt, axis=1))
            grad_k.append(dk)
            grad_v.append(dv)
        contexts.append(jnp.concatenate(context_t, axis=0).T.astype(BF))
        dq = jnp.concatenate(query_t, axis=0).T * scale
        dk = jnp.where(first, grad_k[0], grad_k[1])
        dv = jnp.where(first, grad_v[0], grad_v[1])
        mixed_grads.append((dq, dk, dv))
    context = jnp.concatenate(contexts, axis=0)
    dq, dk, dv = (jnp.concatenate([m[n] for m in mixed_grads], axis=0) for n in range(3))
    grad_mixed = jnp.concatenate([turn(dq, -1.0), turn(dk, -1.0), dv], axis=1).astype(BF)
    total = jnp.sum(grad_mixed.astype(F32), axis=0, keepdims=True)
    for ref, side in ((keep, x), (send, 1 - x)):
        g = mm(normed[:, pl.ds(pl.multiple_of(side * half, half), half)], grad_mixed, TN).astype(BF)
        for t in range(3):
            ref[t, :, pl.ds(pl.multiple_of(p * pair, pair), pair)] = g[:, t * pair : (t + 1) * pair]
    for t in range(3):
        colsum[:, lanes(t)] = total[:, t * pair : (t + 1) * pair]
    g = mm(context, cot[...], TN).astype(BF)
    low_row = pl.multiple_of(lax.rem(p, 2) * pair, pair)

    def store_out(ref):
        for h in range(2):
            ref[3, pl.ds(low_row + h * (half // 2), pair), :] = g[:, h * half : (h + 1) * half]

    @pl.when(p // 2 == x)
    def _():
        store_out(keep)

    @pl.when(p // 2 != x)
    def _():
        store_out(send)

    @pl.when(p == 0)
    def _():
        result[...] = mm(context, wo)
        grad_normed[...] = mm(grad_mixed, w, NT)

    @pl.when(p != 0)
    def _():
        result[...] += mm(context, wo)
        grad_normed[...] += mm(grad_mixed, w, NT)


def norm_kernel(tokens, gains, one, two):
    rows = tokens[...].astype(F32)
    centred = rows - jnp.mean(rows, axis=-1, keepdims=True)
    unit = centred * lax.rsqrt(jnp.mean(centred * centred, axis=-1, keepdims=True) + EPSILON)
    one[...] = (unit * gains[0:1, :] + gains[1:2, :]).astype(BF)
    two[...] = (unit * gains[2:3, :] + gains[3:4, :]).astype(BF)


def tail_kernel(tokens, gains, grad_one, grad_two, sums, send, keep):
    i = pl.program_id(0)
    steps = pl.num_programs(0)
    rows = tokens[...].astype(F32)
    centred = rows - jnp.mean(rows, axis=-1, keepdims=True)
    unit = centred * lax.rsqrt(jnp.mean(centred * centred, axis=-1, keepdims=True) + EPSILON)
    one, two = grad_one[...], grad_two[...]
    part = jnp.concatenate(
        [jnp.sum(v, axis=0, keepdims=True) for v in (one * unit, one, two * unit, two)], axis=0
    )
    pulled = one * gains[0:1, :] + two * gains[2:3, :]

    @pl.when(i == 0)
    def _():
        sums[...] = part

    @pl.when(i != 0)
    def _():
        sums[...] += part

    @pl.when(i < steps // 2)
    def _():
        send[...] = pulled

    @pl.when(i >= steps // 2)
    def _():
        keep[...] = pulled


def halve_kernel(index, keep, recv, send_out, keep_out):
    bit = index[0]
    keep_out[...] = (keep[:, :, bit].astype(F32) + recv[:, :, bit].astype(F32)).astype(BF)
    send_out[...] = (keep[:, :, 1 - bit].astype(F32) + recv[:, :, 1 - bit].astype(F32)).astype(BF)


def widen_kernel(piece, out):
    out[...] = piece[...].astype(F32).reshape(out.shape)


def widen_kernel_at(index, piece, out):
    out[...] = piece[...].astype(F32).reshape(out.shape)


def build(reps):
    bits = reps.bit_length() - 1
    order = list(range(1, bits))

    def flip(array, bit):
        return lax.ppermute(array, "rep", [(i, i ^ (1 << bit)) for i in range(reps)])

    def flip_x(array):
        return lax.ppermute(array, "shard", [(0, 1), (1, 0)])

    def on_device(
        tokens, segments, norm1_gain, norm1_shift, norm2_gain, norm2_shift, qkv_weight, qkv_bias,
        out_weight, out_bias, up_weight, up_bias, down_weight, down_bias, cotangent,
    ):
        half, width = out_weight.shape
        length = tokens.shape[0]
        ff_half = down_weight.shape[0]
        units = ff_half // 2
        toks = 2 * length
        xi = lax.axis_index("shard").astype(jnp.int32)
        ri = lax.axis_index("rep").astype(jnp.int32)
        rbit = [(ri >> b) & 1 for b in range(bits)]
        ci = rbit[0]
        index = jnp.stack([xi, ci, rbit[1], rbit[2]])

        def call(kernel, grid, in_specs, out_specs, out_shape, scratch=(), mib=32, est=None):
            return pl.pallas_call(
                kernel,
                grid_spec=pltpu.PrefetchScalarGridSpec(
                    num_scalar_prefetch=1,
                    grid=grid,
                    in_specs=in_specs,
                    out_specs=out_specs,
                    scratch_shapes=list(scratch),
                ),
                out_shape=out_shape,
                compiler_params=params(mib),
                cost_estimate=est,
            )

        up_part = call(
            pack_up_kernel, (), [ANY], ANY, sds((half // 4, 2 * units), BF),
            [pltpu.SemaphoreType.DMA((2,))],
        )(index, up_weight)
        down_part, rest_part = call(
            pack_rest_kernel, (), [ANY] * 3, [ANY] * 2,
            [sds((units // 4, width), BF), sds((half // 4, 4 * half), BF)],
            [pltpu.SemaphoreType.DMA((9,))],
        )(index, down_weight, qkv_weight, out_weight)

        def fetch(part):
            own = flip_x(part)
            over_y = flip(own, 1)
            return own, over_y, flip(own, 2), flip(over_y, 2)

        def lay(vector, rows, at, total):
            v = vector.astype(F32).reshape(rows, half)
            return jnp.pad(v, ((at, total - at - rows), (0, 0)))

        small_own = (
            lay(norm1_gain, 1, 0, 13) + lay(norm1_shift, 1, 1, 13) + lay(norm2_gain, 1, 2, 13)
            + lay(norm2_shift, 1, 3, 13) + lay(out_bias, 1, 4, 13) + lay(down_bias, 1, 5, 13)
            + lay(qkv_bias, 3, 6, 13) + lay(up_bias, 4, 9, 13)
        )
        small_other = flip_x(small_own)
        tokens_other = flip(tokens, 0)
        up_pieces = fetch(up_part)
        cot_other = flip(cotangent, 0)
        segments_other = flip(segments, 0)
        down_pieces = fetch(down_part)
        rest_pieces = fetch(rest_part)

        low = jnp.where(xi == 0, small_own, small_other)
        high = jnp.where(xi == 0, small_other, small_own)
        gains = jnp.concatenate([low[:6], high[:6]], axis=1)
        qkv_b = jnp.concatenate([low[6:9], high[6:9]], axis=0).reshape(3, 2, 2, half // 2)
        qkv_b = lax.dynamic_index_in_dim(qkv_b, ci, 2, keepdims=False).reshape(1, 3 * half)
        up_b = jnp.concatenate([low[9:13], high[9:13]], axis=0).reshape(2, 2, units)
        up_b = lax.dynamic_index_in_dim(up_b, ci, 1, keepdims=False)
        up_b_own = lax.dynamic_slice_in_dim(up_b, xi, 1, 0)
        up_b_other = lax.dynamic_slice_in_dim(up_b, 1 - xi, 1, 0)

        both = jnp.concatenate([tokens, tokens_other], 0)
        cot = jnp.concatenate([cotangent, cot_other], 0)
        rows = 256
        normed_one, normed_two = pl.pallas_call(
            norm_kernel,
            grid=(toks // rows,),
            in_specs=[pl.BlockSpec((rows, width), lambda i: (i, 0)), held((6, width))],
            out_specs=[pl.BlockSpec((rows, width), lambda i: (i, 0))] * 2,
            out_shape=[sds((toks, width), BF)] * 2,
            compiler_params=params(24),
            cost_estimate=cost(20 * toks * width, 6 * toks * width),
        )(both, gains)

        steps = units // BLOCK
        column = pl.BlockSpec((toks, BLOCK), lambda j, *_: (0, j))
        bias_block = pl.BlockSpec((1, BLOCK), lambda j, *_: (0, j))
        down_block = pl.BlockSpec((2, BLOCK, TILE), lambda j, *_: (j // 2, j % 2, 0))
        up_block = pl.BlockSpec((1, TILE, BLOCK), lambda j, *_: (j // 2, 0, j % 2))
        four = sds((4, TILE, TILE), BF)
        two = sds((2, TILE, TILE), BF)
        unit_act = sds((toks, units), BF)
        full = held((toks, width))
        w_scratch = pltpu.VMEM((width, units), BF)
        one_mm = 2 * toks * width * units
        act_x, slope_x, down_send = call(
            ffn_other_kernel, (steps,), [full, full, bias_block] + [ANY] * 5,
            [column, column, down_block], [unit_act, unit_act, four],
            [w_scratch, pltpu.SemaphoreType.DMA((5,))], 40, cost(2 * one_mm, 14 * MIB),
        )(index, normed_two, cot, up_b_other, up_weight, *up_pieces)
        act_o, hid_o, down_keep, up_send_o, up_keep_o, colsum_o = call(
            ffn_own_kernel, (steps,),
            [full, full, bias_block, pl.BlockSpec((BLOCK, width), lambda j, i: (i[1] * steps + j, 0))] + [ANY] * 5,
            [column, column, down_block, up_block, up_block, bias_block],
            [unit_act, unit_act, four, two, two, sds((1, units), F32)],
            [w_scratch, pltpu.SemaphoreType.DMA((5,))], 40, cost(4 * one_mm, 18 * MIB),
        )(index, normed_two, cot, up_b_own, down_weight, up_weight, *up_pieces)
        hid_x, up_send_x, up_keep_x, colsum_x = call(
            ffn_back_kernel, (steps,), [full, full, column] + [ANY] * 4,
            [column, up_block, up_block, bias_block],
            [unit_act, two, two, sds((1, units), F32)],
            [pltpu.VMEM((units, width), BF), pltpu.SemaphoreType.DMA((4,))], 40, cost(2 * one_mm, 14 * MIB),
        )(index, normed_two, cot, slope_x, *down_pieces)
        token_rows = pl.BlockSpec((rows, units), lambda i, *_: (i, 0))
        token_out = pl.BlockSpec((rows, width), lambda i, *_: (i, 0))
        wide_f32 = sds((toks, width), F32)
        ffn_part, grad_two = call(
            ffn_last_kernel, (toks // rows,), [token_rows] * 4 + [ANY] * 10, [token_out] * 2, [wide_f32] * 2,
            [w_scratch, w_scratch, pltpu.VMEM((units, width), BF), pltpu.VMEM((units, width), BF),
             pltpu.SemaphoreType.DMA((15,))], 40, cost(4 * one_mm, 24 * MIB),
        )(index, act_o, act_x, hid_o, hid_x, down_weight, *down_pieces, up_weight, *up_pieces)

        documents = jnp.concatenate([segments, segments_other], 0)
        before = jnp.sum((documents[:, None, :] < documents[:, :, None]).astype(jnp.int32), axis=2)
        offsets = (jnp.arange(length, dtype=jnp.int32)[None] - before).astype(F32).reshape(toks, 1)
        inverse = 1.0 / 10000.0 ** (jnp.arange(0, ROT, 2, dtype=F32) / ROT)
        angles = offsets * inverse[None, :]
        cos8, sin8 = jnp.cos(angles), jnp.sin(angles)
        rest = jnp.ones((toks, HD - ROT), F32)
        none8 = jnp.zeros((toks, ROT // 2), F32)
        cosine = jnp.concatenate([cos8, cos8, rest] * 2, axis=1)
        sine_low = jnp.concatenate([-sin8, none8, 0.0 * rest] * 2, axis=1)
        sine_high = jnp.concatenate([none8, sin8, 0.0 * rest] * 2, axis=1)

        pair = 2 * HD
        table = held((toks, pair))
        rest_send, rest_keep, grad_one, attn_part, colsum_q = call(
            attention_kernel, (half // pair,),
            [full, full, table, table, table, held((toks, 1)), held((2, length)), held((1, 3 * half))] + [ANY] * 6,
            [held((4, TILE, TILE)), held((4, TILE, TILE)), full, full, held((1, 3 * half))],
            [four, four, wide_f32, wide_f32, sds((1, 3 * half), F32)],
            [pltpu.VMEM((width, 3 * half), BF), pltpu.VMEM((half, width), BF),
             pltpu.VMEM((2, length, length), F32), pltpu.SemaphoreType.DMA((19,))],
            56, cost(13e9 + 20e9, 24 * MIB),
        )(
            index, normed_one, cot, cosine, sine_low, sine_high, documents.reshape(toks, 1), documents, qkv_b,
            qkv_weight, out_weight, *rest_pieces,
        )

        def halve(keep, recv, bit):
            n, r, cols = keep.shape
            m = (reps // 2) >> bit
            small = r // (2 * m)
            view = (n, m, 2, small, cols)
            block = pl.BlockSpec((1, m, 2, small, cols), lambda t, *_: (t, 0, 0, 0, 0))
            out_block = pl.BlockSpec((1, m, small, cols), lambda t, *_: (t, 0, 0, 0))
            send_next, keep_next = call(
                halve_kernel, (n,), [block, block], [out_block] * 2, [sds((n, m, small, cols), BF)] * 2,
                (), 24, cost(2 * n * r * cols, 6 * n * r * cols),
            )(rbit[bit].reshape(1), keep.reshape(view), recv.reshape(view))
            return send_next.reshape(n, r // 2, cols), keep_next.reshape(n, r // 2, cols)

        def reduce_scatter(keep, recv):
            for bit in order:
                send, keep = halve(keep, recv, bit)
                recv = flip(send, bit)
            return (keep.astype(F32) + recv.astype(F32)).astype(BF)

        recv_down = flip_x(down_send)
        recv_up_x = flip_x(up_send_o)
        recv_up_o = flip_x(up_send_x)
        recv_rest = flip_x(rest_send)
        down_piece = reduce_scatter(down_keep, recv_down)
        up_piece_x = reduce_scatter(up_keep_x, recv_up_x)
        up_piece_o = reduce_scatter(up_keep_o, recv_up_o)
        rest_piece = reduce_scatter(rest_keep, recv_rest)
        first_piece = jnp.concatenate([down_piece, up_piece_o, up_piece_x], axis=0)
        r = first_piece.shape[1]
        first = lax.all_gather(first_piece, "rep", axis=0, tiled=False).reshape(reps // 2, 2, 8, r, TILE)
        second = lax.all_gather(rest_piece, "rep", axis=0, tiled=False).reshape(reps // 2, 2, 4, r, TILE)

        many = reps // 2
        down_grad = pl.pallas_call(
            widen_kernel, grid=(2, 2, 2),
            in_specs=[pl.BlockSpec((many, 1, 1, r, TILE), lambda c, i, j: (0, c, 2 * i + j, 0, 0))],
            out_specs=pl.BlockSpec((TILE, TILE), lambda c, i, j: (2 * c + i, j)),
            out_shape=sds((ff_half, width), F32), compiler_params=params(24),
            cost_estimate=cost(ff_half * width, 6 * ff_half * width),
        )(first)
        up_grad = call(
            widen_kernel_at, (2, 2, 2),
            [pl.BlockSpec((many, 1, 1, r, TILE), lambda c, o, j, i: (0, c, 4 + 2 * o + j, 0, 0))],
            pl.BlockSpec((TILE, TILE), lambda c, o, j, i: (0, 4 * (i[0] ^ o) + 2 * c + j)),
            sds((half, 2 * ff_half), F32), (), 24, cost(ff_half * width, 6 * ff_half * width),
        )(index, first)
        qkv_grad = pl.pallas_call(
            widen_kernel, grid=(2, 3, 2),
            in_specs=[pl.BlockSpec((many, 1, 1, r, half // 2), lambda c, t, h: (0, c, t, 0, h))],
            out_specs=pl.BlockSpec((half, half // 2), lambda c, t, h: (0, 4 * t + 2 * h + c)),
            out_shape=sds((half, 6 * half), F32), compiler_params=params(24),
            cost_estimate=cost(half * width, 6 * half * 6 * half),
        )(second)
        out_grad = pl.pallas_call(
            widen_kernel, grid=(2, 2),
            in_specs=[pl.BlockSpec((many // 2, 1, 1, r, TILE), lambda c, h: (h, c, 3, 0, 0))],
            out_specs=pl.BlockSpec((half // 2, half), lambda c, h: (c, h)),
            out_shape=sds((half, width), F32), compiler_params=params(24),
            cost_estimate=cost(half * width, 6 * half * width),
        )(second)

        part = ffn_part + attn_part
        output = (
            tokens.astype(F32) + (part[:length] + flip(part[length:], 0)) + (gains[4:5] + gains[5:6])
        ).astype(BF)
        blocks = toks // rows

        def turned(i):
            return ((i + blocks // 2) % blocks, 0)

        row_block = pl.BlockSpec((rows, width), turned)
        sums, pulled_send, pulled_keep = pl.pallas_call(
            tail_kernel,
            grid=(blocks,),
            in_specs=[row_block, held((6, width)), row_block, row_block],
            out_specs=[
                pl.BlockSpec((4, width), lambda i: (0, 0)),
                pl.BlockSpec((rows, width), lambda i: (jnp.minimum(i, blocks // 2 - 1), 0)),
                pl.BlockSpec((rows, width), lambda i: (jnp.maximum(i - blocks // 2, 0), 0)),
            ],
            out_shape=[sds((4, width), F32), sds((length, width), F32), sds((length, width), F32)],
            compiler_params=params(32),
            cost_estimate=cost(20 * toks * width, 14 * toks * width),
        )(both, gains, grad_one, grad_two)
        pulled = pulled_keep + flip(pulled_send, 0)
        own_rows = tokens.astype(F32)
        centred = own_rows - jnp.mean(own_rows, axis=-1, keepdims=True)
        spread = lax.rsqrt(jnp.mean(centred * centred, axis=-1, keepdims=True) + EPSILON)
        unit = centred * spread
        inward = spread * (
            pulled
            - jnp.mean(pulled, axis=-1, keepdims=True)
            - unit * jnp.mean(pulled * unit, axis=-1, keepdims=True)
        )
        grad_tokens = (cotangent.astype(F32) + inward).astype(BF)

        def spread_core(vector, parts):
            size = vector.size // parts
            v = vector.reshape(parts, 1, size)
            keep = (jnp.arange(2) == ci)[None, :, None]
            return jnp.where(keep, v, 0.0).reshape(-1, width)

        column_sum = jnp.sum(cotangent.astype(F32), axis=0, keepdims=True)
        colsum_up = jnp.where(
            xi == 0, jnp.concatenate([colsum_o, colsum_x], 0), jnp.concatenate([colsum_x, colsum_o], 0)
        )
        small = jnp.concatenate([sums, column_sum, spread_core(colsum_q, 6), spread_core(colsum_up, 2)], axis=0)
        small = small + flip_x(small)
        for bit in range(bits):
            small = small + flip(small, bit)

        def owned(row, count=1):
            v = small[row : row + count].reshape(2, -1)
            return lax.dynamic_index_in_dim(v, xi, 0, keepdims=False)

        bias_out = owned(4)
        return (
            output, grad_tokens, owned(0), owned(1), owned(2), owned(3), qkv_grad, owned(5, 3),
            out_grad, bias_out, up_grad, owned(8, 4), down_grad, bias_out,
        )

    return on_device


def solution(mesh):
    both = P(("rep", "shard"), None)
    vector = P("shard")
    matrix = P("shard", None)
    weights = (
        vector, vector, vector, vector, matrix, vector, matrix, vector, matrix, vector, matrix, vector,
    )
    return jax.shard_map(
        build(mesh.shape["rep"]),
        mesh=mesh,
        in_specs=(both, both) + weights + (both,),
        out_specs=(both, both) + weights,
        check_vma=False,
    )
```

time: 681 us -> 533 us (0.78); the launches traced: 670 us -> 531 us
  Pallas kernels: 0 us -> 148 us
  matrix products: 118 us -> 0 us
  local copies, waits for them, and re-layouts: 168 us -> 69.5 us
  other arithmetic: 116 us -> 19.3 us
  waiting for transfers between devices: 214 us -> 229 us
  between operations: 2.55 us -> 14.8 us
    pallas_call x0 -> x25, Pallas kernels: none -> 148 us  [the longest x1 59 us: on_device(): call(attention_kernel, (half // pair,), [full, full, table, table, table,...]
    dot_general x21 -> x0, matrix products: 107 us -> none  [the longest x16 79.4 us: dot(): lax.dot_general(left, right, (((left_dim,), (right_dim,)), ((), ())), pre...]
    convert_element_type x23 -> x4, other arithmetic: 60 us -> 0.91 us  [reduce_scatter(): return (keep.astype(F32) + recv.astype(F32)).astype(BF)]
    ppermute x10 -> x9, waiting for transfers between devices: 44.1 us -> 86.5 us  [flip_x(): return lax.ppermute(array, 'shard', [(0, 1), (1, 0)])]
    select_n x32 -> x4, other arithmetic: 38 us -> 0.21 us  [the longest x2 0.15 us: spread_core(): return jnp.where(keep, v, 0.0).reshape(-1, width)]
    ppermute x41 -> x30, waiting for transfers between devices: 170 us -> 142 us  [flip(): return lax.ppermute(array, 'rep', [(i, i ^ 1 << bit) for i in range(reps)])]
    convert_element_type x4 -> x0, local copies, waits for them, and re-layouts: 25.1 us -> none  [the longest x1 11.8 us: on_device(): jnp.transpose(up_all, (1, 2, 0, 3)).reshape(half, 2 * ff_half).astype(F32)]
    slice x16 -> x9, local copies, waits for them, and re-layouts: 15.1 us -> 0.09 us  [the longest x3 0.07 us: owned(): v = small[row:row + count].reshape(2, -1)]
  transfers between devices with their start and end apart: 51 -> 41, of which waited for: 22 -> 26; matrix products, arithmetic and copies ran while one was open for 56% -> 8% of each run, Pallas kernels for 0% -> 14%
where the time goes in v2:
time: 533 us; the launch traced here: 531 us
  waiting for transfers between devices  229 us (43%)
  Pallas kernels  148 us (28%)
  local copies, waits for them, and re-layouts  69.5 us (13%)
  starting transfers between devices  51.1 us (10%)
  other arithmetic  19.3 us (4%)
  between operations  14.8 us (3%)
    ppermute x30, waiting for transfers between devices, flip(): return lax.ppermute(array, 'rep', [(i, i ^ 1 << bit) for i in range(reps)])  142 us
    ppermute x9, waiting for transfers between devices, flip_x(): return lax.ppermute(array, 'shard', [(0, 1), (1, 0)])  86.5 us
    pallas_call x1, Pallas kernels, on_device(): call(attention_kernel, (half // pair,), [full, full, table, table, table,...  59 us
    unnamed x106, local copies, waits for them, and re-layouts  46.4 us
    ppermute x30, starting transfers between devices, flip(): return lax.ppermute(array, 'rep', [(i, i ^ 1 << bit) for i in range(reps)])  40.5 us
    pallas_call x1, Pallas kernels, on_device(): call(ffn_own_kernel, (steps,), [full, full, bias_block, pl.BlockSpec((BLO...  19.3 us
    pallas_call x1, Pallas kernels, on_device(): call(ffn_last_kernel, (toks // rows,), [token_rows] * 4 + [ANY] * 10, [to...  14.5 us
    pallas_call x1, Pallas kernels, on_device(): call(ffn_other_kernel, (steps,), [full, full, bias_block] + [ANY] * 5, [c...  13.6 us
  transfers between devices with their start and end apart: 41, of which 26 were waited for; matrix products, arithmetic and copies ran while one was open for 8% of the time, Pallas kernels for 14%

profile of v2, /device:TPU:0, one launch (start us, length us, event | category | flops | bytes accessed | tf_op | source)
XLA Modules:
  0.0 531.5 jit_solution(18404966599209544084)
XLA Ops:
  25.9 11.5 %collective-permute-done.12.p0 = bf16[128,2048]{1,0:T(8,128)(2,1)} collective-permute-done((bf16[128,2048]{1,0:T(8,128)(2,1)S(1)}, bf16[128,2048]{1,0:T(8,128)(2,1)}, u32[]{:S(2)}, u32[]{:S(2)}) %collective-permute-start.12) | collective-permute-done | bytes 524320 | tf_op jit(solution)/shard_map/ppermute | solution.py:431
  61.5 5.5 %collective-permute-done.14.p2 = bf16[128,2048]{1,0:T(8,128)(2,1)S(1)} collective-permute-done((bf16[128,2048]{1,0:T(8,128)(2,1)}, bf16[128,2048]{1,0:T(8,128)(2,1)S(1)}, u32[]{:S(2)}, u32[]{:S(2)}) %collective-permute-start.14) | collective-permute-done | bytes 524320 | tf_op jit(solution)/shard_map/ppermute | solution.py:428
  67.1 9.3 %collective-permute-done.15.p3 = bf16[128,2048]{1,0:T(8,128)(2,1)S(1)} collective-permute-done((bf16[128,2048]{1,0:T(8,128)(2,1)}, bf16[128,2048]{1,0:T(8,128)(2,1)S(1)}, u32[]{:S(2)}, u32[]{:S(2)}) %collective-permute-start.15) | collective-permute-done | bytes 524320 | tf_op jit(solution)/shard_map/ppermute | solution.py:428
  77.2 59.0 %shard_map.261 = (bf16[4,512,512]{2,1,0:T(8,128)(2,1)}, bf16[4,512,512]{2,1,0:T(8,128)(2,1)}, f32[1024,1024]{1,0:T(8,128)}, f32[1024,1024]{1,0:T(8,128)}, f32[1,1536]{1,0:T(1,128)}) custom-call(s32[4]{0:T(128)} %copy-done.15, bf16[1024,1024]{1,0:T(8,128)(2,1)} %copy-done.19, bf16[1024,1024]{1,0:T(8,128)(2,1)} %copy-done.12, f32[1024,128]{1,0:T(8,128)} %concatenate.52.cosine, ...), custom_call_target="tpu_custom_call" | custom-call | flops 32999999488 | bytes 25165824 | tf_op jit(solution)/shard_map/pallas_call | solution.py:570
  136.9 45.4 %collective-permute-done.23 = bf16[4,512,512]{2,1,0:T(8,128)(2,1)S(1)} collective-permute-done((bf16[4,512,512]{2,1,0:T(8,128)(2,1)}, bf16[4,512,512]{2,1,0:T(8,128)(2,1)S(1)}, u32[]{:S(2)}, u32[]{:S(2)}) %collective-permute-start.23) | collective-permute-done | bytes 2097184 | tf_op jit(solution)/shard_map/ppermute | solution.py:431
  184.9 21.8 %collective-permute-done.24 = bf16[4,256,512]{2,1,0:T(8,128)(2,1)S(1)} collective-permute-done((bf16[4,256,512]{2,1,0:T(8,128)(2,1)S(1)}, bf16[4,256,512]{2,1,0:T(8,128)(2,1)S(1)}, u32[]{:S(2)}, u32[]{:S(2)}) %collective-permute-start.24) | collective-permute-done | bytes 1048608 | tf_op jit(solution)/shard_map/ppermute | solution.py:428
  209.8 10.6 %collective-permute-done.25 = bf16[4,128,512]{2,1,0:T(8,128)(2,1)S(1)} collective-permute-done((bf16[4,128,512]{2,1,0:T(8,128)(2,1)}, bf16[4,128,512]{2,1,0:T(8,128)(2,1)S(1)}, u32[]{:S(2)}, u32[]{:S(2)}) %collective-permute-start.25) | collective-permute-done | bytes 524320 | tf_op jit(solution)/shard_map/ppermute | solution.py:428
  223.2 7.4 %collective-permute-done.26 = bf16[4,64,512]{2,1,0:T(8,128)(2,1)S(1)} collective-permute-done((bf16[4,64,512]{2,1,0:T(8,128)(2,1)S(1)}, bf16[4,64,512]{2,1,0:T(8,128)(2,1)S(1)}, u32[]{:S(2)}, u32[]{:S(2)}) %collective-permute-start.26) | collective-permute-done | bytes 262176 | tf_op jit(solution)/shard_map/ppermute | solution.py:428
  235.1 8.6 %collective-permute-done.3.p0 = bf16[128,2048]{1,0:T(8,128)(2,1)S(1)} collective-permute-done((bf16[128,2048]{1,0:T(8,128)(2,1)S(1)}, bf16[128,2048]{1,0:T(8,128)(2,1)S(1)}, u32[]{:S(2)}, u32[]{:S(2)}) %collective-permute-start.3) | collective-permute-done | bytes 524320 | tf_op jit(solution)/shard_map/ppermute | solution.py:431
  244.2 8.8 %collective-permute-done.4.p1 = bf16[128,2048]{1,0:T(8,128)(2,1)} collective-permute-done((bf16[128,2048]{1,0:T(8,128)(2,1)S(1)}, bf16[128,2048]{1,0:T(8,128)(2,1)}, u32[]{:S(2)}, u32[]{:S(2)}) %collective-permute-start.4) | collective-permute-done | bytes 524320 | tf_op jit(solution)/shard_map/ppermute | solution.py:428
  253.7 9.5 %collective-permute-done.5.p2 = bf16[128,2048]{1,0:T(8,128)(2,1)} collective-permute-done((bf16[128,2048]{1,0:T(8,128)(2,1)S(1)}, bf16[128,2048]{1,0:T(8,128)(2,1)}, u32[]{:S(2)}, u32[]{:S(2)}) %collective-permute-start.5) | collective-permute-done | bytes 524320 | tf_op jit(solution)/shard_map/ppermute | solution.py:428
  263.2 22.6 %collective-permute-done.6.p3 = bf16[128,2048]{1,0:T(8,128)(2,1)} collective-permute-done((bf16[128,2048]{1,0:T(8,128)(2,1)}, bf16[128,2048]{1,0:T(8,128)(2,1)}, u32[]{:S(2)}, u32[]{:S(2)}) %collective-permute-start.6) | collective-permute-done | bytes 524320 | tf_op jit(solution)/shard_map/ppermute | solution.py:428
  289.1 13.6 %shard_map.257 = (bf16[1024,1024]{1,0:T(8,128)(2,1)S(1)}, bf16[1024,1024]{1,0:T(8,128)(2,1)S(1)}, bf16[4,512,512]{2,1,0:T(8,128)(2,1)}) custom-call(s32[4]{0:T(128)S(1)} %copy-done.16, bf16[1024,1024]{1,0:T(8,128)(2,1)S(1)} %copy-done.18, bf16[1024,1024]{1,0:T(8,128)(2,1)S(1)} %copy-done.13, f32[1,1024]{1,0:T(1,128)S(1)} %get-tuple-element.129.bias, ...), custom_call_target="tpu_custom_call" | custom-call | flops 4294967296 | bytes 14680064 | tf_op jit(solution)/shard_map/pallas_call | solution.py:529
  306.4 8.7 %collective-permute-done.8.d1 = bf16[256,1024]{1,0:T(8,128)(2,1)S(1)} collective-permute-done((bf16[256,1024]{1,0:T(8,128)(2,1)}, bf16[256,1024]{1,0:T(8,128)(2,1)S(1)}, u32[]{:S(2)}, u32[]{:S(2)}) %collective-permute-start.8) | collective-permute-done | bytes 524320 | tf_op jit(solution)/shard_map/ppermute | solution.py:428
  315.0 19.3 %shard_map.256 = (bf16[1024,1024]{1,0:T(8,128)(2,1)S(1)}, bf16[1024,1024]{1,0:T(8,128)(2,1)S(1)}, bf16[4,512,512]{2,1,0:T(8,128)(2,1)S(1)}, bf16[2,512,512]{2,1,...) custom-call(s32[4]{0:T(128)S(1)} %copy-done.16, bf16[1024,1024]{1,0:T(8,128)(2,1)S(1)} %copy-done.18, ...), custom_call_target="tpu_custom_call" | custom-call | flops 8589934592 | bytes 18874368 | tf_op jit(solution)/shard_map/pallas_call | solution.py:534
  340.8 11.6 %shard_map.259 = (bf16[1024,1024]{1,0:T(8,128)(2,1)S(1)}, bf16[2,512,512]{2,1,0:T(8,128)(2,1)S(1)}, bf16[2,512,512]{2,1,0:T(8,128)(2,1)S(1)}, f32[1,1024]{1,0:T(1,128)S(1)}) custom-call(s32[4]{0:T(128)S(1)} %copy-done.16, bf16[1024,1024]{1,0:T(8,128)(2,1)S(1)} %copy-done.18, bf16[1024,1024]{1,0:T(8,128)(2,1)S(1)} %copy-done.14, ...), custom_call_target="tpu_custom_call" | custom-call | flops 4294967296 | bytes 14680064 | tf_op jit(solution)/shard_map/pallas_call | solution.py:541
  355.5 8.8 %collective-permute-done.35 = bf16[2,512,512]{2,1,0:T(8,128)(2,1)S(1)} collective-permute-done((bf16[2,512,512]{2,1,0:T(8,128)(2,1)}, bf16[2,512,512]{2,1,0:T(8,128)(2,1)S(1)}, u32[]{:S(2)}, u32[]{:S(2)}) %collective-permute-start.35) | collective-permute-done | bytes 1048608 | tf_op jit(solution)/shard_map/ppermute | solution.py:431
  365.8 9.8 %collective-permute-done.31 = bf16[2,512,512]{2,1,0:T(8,128)(2,1)S(1)} collective-permute-done((bf16[2,512,512]{2,1,0:T(8,128)(2,1)S(1)}, bf16[2,512,512]{2,1,0:T(8,128)(2,1)S(1)}, u32[]{:S(2)}, u32[]{:S(2)}) %collective-permute-start.31) | collective-permute-done | bytes 1048608 | tf_op jit(solution)/shard_map/ppermute | solution.py:431
  382.9 3.5 collective-permute-done.32
  388.5 5.0 collective-permute-done.37
  393.7 11.5 %collective-permute-start.38 = (bf16[2,64,512]{2,1,0:T(8,128)(2,1)S(1)}, bf16[2,64,512]{2,1,0:T(8,128)(2,1)S(1)}, u32[]{:S(2)}, u32[]{:S(2)}) collective-permute-start(bf16[2,64,512]{2,1,0:T(8,128)(2,1)S(1)} %bitcast.113), channel_id=1, source_target_pairs={{0,16},{2,18},{4,20},{6,22},{8,24},{10,26},{12,28},{14,30},{16,0},... | collective-permute-start | bytes 393224 | tf_op jit(solution)/shard_map/ppermute | solution.py:428
  412.6 5.7 %collective-permute-done.30 = bf16[4,64,512]{2,1,0:T(8,128)(2,1)S(1)} collective-permute-done((bf16[4,64,512]{2,1,0:T(8,128)(2,1)S(1)}, bf16[4,64,512]{2,1,0:T(8,128)(2,1)S(1)}, u32[]{:S(2)}, u32[]{:S(2)}) %collective-permute-start.30) | collective-permute-done | bytes 262176 | tf_op jit(solution)/shard_map/ppermute | solution.py:428
  428.8 14.5 %shard_map.260 = (f32[1024,1024]{1,0:T(8,128)}, f32[1024,1024]{1,0:T(8,128)}) custom-call(s32[4]{0:T(128)S(1)} %copy-done.16, bf16[1024,1024]{1,0:T(8,128)(2,1)S(1)} %copy-done.34, bf16[1024,1024]{1,0:T(8,128)(2,1)S(1)} %copy-done.28, bf16[1024,1024]{1,0:T(8,128)(2,1)S(1)} %copy-done.36, bf16[1024,1024]{1,0:T(8,128)(2,1)S(1)} %copy-done.32, ...), custom_call_target="tpu_custom_call" | custom-call | flops 8589934592 | bytes 25165824 | tf_op jit(solution)/shard_map/pallas_call | solution.py:550
  445.6 4.6 shard_map.262
  453.0 5.4 %add.142 = f32[1024,1024]{1,0:T(8,128)S(1)} add(f32[1024,1024]{1,0:T(8,128)} %get-tuple-element.72, f32[1024,1024]{1,0:T(8,128)} %get-tuple-element.75) | non-fusion elementwise | flops 1048576 | bytes 12582912 | tf_op jit(solution)/shard_map/add | solution.py:644
  466.7 3.4 convert_reduce_fusion.1
  482.4 7.3 %collective-permute-done.21 = f32[12,1024]{1,0:T(8,128)S(1)} collective-permute-done((f32[12,1024]{1,0:T(8,128)S(1)}, f32[12,1024]{1,0:T(8,128)S(1)}, u32[]{:S(2)}, u32[]{:S(2)}) %collective-permute-start.21) | collective-permute-done | bytes 49184 | tf_op jit(solution)/shard_map/ppermute | solution.py:428
  491.6 6.6 %collective-permute-done.22 = f32[12,1024]{1,0:T(8,128)S(1)} collective-permute-done((f32[12,1024]{1,0:T(8,128)S(1)}, f32[12,1024]{1,0:T(8,128)S(1)}, u32[]{:S(2)}, u32[]{:S(2)}) %collective-permute-start.22) | collective-permute-done | bytes 49184 | tf_op jit(solution)/shard_map/ppermute | solution.py:428
  503.6 5.3 shard_map.266
  510.7 3.4 copy-done
  514.1 5.2 shard_map.277
  519.4 4.7 shard_map.278
  (268 shorter events, 138.8 us)
Async XLA Ops:
  7.2 494.2 %all-gather.5.cloned.1.call-start = ((), (), s32[]{:S(2)}) async-start(), calls=%async_computation | async-start | bytes 4456448 | tf_op jit(solution)/shard_map/all_gather | solution.py:613
  7.2 47.5 %collective-permute-start = (bf16[512,1024]{1,0:T(8,128)(2,1)}, bf16[512,1024]{1,0:T(8,128)(2,1)}, u32[]{:S(2)}, u32[]{:S(2)}) collective-permute-start(bf16[512,1024]{1,0:T(8,128)(2,1)} %param.15), channel_id=1, source_target_pairs={{0,2},{2,0},{4,6},{6,4},{8,10},{10,8},{12,14},{14,12},{16,18},{18,... | collective-permute-start | bytes 3145736 | tf_op jit(solution)/shard_map/ppermute | solution.py:428
  13.3 38.6 %collective-permute-start.1 = (f32[13,512]{1,0:T(8,128)S(1)}, f32[13,512]{1,0:T(8,128)S(1)}, u32[]{:S(2)}, u32[]{:S(2)}) collective-permute-start(f32[13,512]{1,0:T(8,128)S(1)} %convert_add_fusion.6), channel_id=1, source_target_pairs={{0,1},{1,0},{2,3},{3,2},{4,5},{5,4},{6,7},{7,6},{8,9},{9,8},{10,11... | collective-permute-start | bytes 79880 | tf_op jit(solution)/shard_map/ppermute | solution.py:431
  15.8 43.6 %collective-permute-start.2 = (bf16[512,1024]{1,0:T(8,128)(2,1)}, bf16[512,1024]{1,0:T(8,128)(2,1)}, u32[]{:S(2)}, u32[]{:S(2)}) collective-permute-start(bf16[512,1024]{1,0:T(8,128)(2,1)} %param.29), channel_id=1, source_target_pairs={{0,2},{2,0},{4,6},{6,4},{8,10},{10,8},{12,14},{14,12},{16,18},{18,... | collective-permute-start | bytes 3145736 | tf_op jit(solution)/shard_map/ppermute | solution.py:428
  16.1 9.4 %collective-permute-start.11 = (s32[1,512]{1,0:T(1,128)}, s32[1,512]{1,0:T(1,128)S(1)}, u32[]{:S(2)}, u32[]{:S(2)}) collective-permute-start(s32[1,512]{1,0:T(1,128)} %param.16), channel_id=1, source_target_pairs={{0,2},{2,0},{4,6},{6,4},{8,10},{10,8},{12,14},{14,12},{16,18},{18,... | collective-permute-start | bytes 6152 | tf_op jit(solution)/shard_map/ppermute | solution.py:428
  23.2 14.2 %collective-permute-start.12 = (bf16[128,2048]{1,0:T(8,128)(2,1)S(1)}, bf16[128,2048]{1,0:T(8,128)(2,1)}, u32[]{:S(2)}, u32[]{:S(2)}) collective-permute-start(bf16[128,2048]{1,0:T(8,128)(2,1)S(1)} %get-tuple-element.74), channel_id=1, source_target_pairs={{0,1},{1,0},{2,3},{3,2},{4,5},{5,4},{6,7},{7,6},{8,9},{9,8},{10,11... | collective-permute-start | bytes 1572872 | tf_op jit(solution)/shard_map/ppermute | solution.py:431
  37.4 16.1 %collective-permute-start.13 = (bf16[128,2048]{1,0:T(8,128)(2,1)}, bf16[128,2048]{1,0:T(8,128)(2,1)}, u32[]{:S(2)}, u32[]{:S(2)}) collective-permute-start(bf16[128,2048]{1,0:T(8,128)(2,1)} %collective-permute-done.12.p0), channel_id=1, source_target_pairs={{0,4},{2,6},{4,0},{6,2},{8,12},{10,14},{12,8},{14,10},{16,20},{18,... | collective-permute-start | bytes 1572872 | tf_op jit(solution)/shard_map/ppermute | solution.py:428
  51.9 15.1 %collective-permute-start.14 = (bf16[128,2048]{1,0:T(8,128)(2,1)}, bf16[128,2048]{1,0:T(8,128)(2,1)S(1)}, u32[]{:S(2)}, u32[]{:S(2)}) collective-permute-start(bf16[128,2048]{1,0:T(8,128)(2,1)} %collective-permute-done.12.p0), channel_id=1, source_target_pairs={{0,8},{2,10},{4,12},{6,14},{8,0},{10,2},{12,4},{14,6},{16,24},{18,... | collective-permute-start | bytes 1572872 | tf_op jit(solution)/shard_map/ppermute | solution.py:428
  53.6 22.8 %collective-permute-start.15 = (bf16[128,2048]{1,0:T(8,128)(2,1)}, bf16[128,2048]{1,0:T(8,128)(2,1)S(1)}, u32[]{:S(2)}, u32[]{:S(2)}) collective-permute-start(bf16[128,2048]{1,0:T(8,128)(2,1)} %collective-permute-done.13.p1), channel_id=1, source_target_pairs={{0,8},{2,10},{4,12},{6,14},{8,0},{10,2},{12,4},{14,6},{16,24},{18,... | collective-permute-start | bytes 1572872 | tf_op jit(solution)/shard_map/ppermute | solution.py:428
  136.2 46.0 %collective-permute-start.23 = (bf16[4,512,512]{2,1,0:T(8,128)(2,1)}, bf16[4,512,512]{2,1,0:T(8,128)(2,1)S(1)}, u32[]{:S(2)}, u32[]{:S(2)}) collective-permute-start(bf16[4,512,512]{2,1,0:T(8,128)(2,1)} %get-tuple-element.85), channel_id=1, source_target_pairs={{0,1},{1,0},{2,3},{3,2},{4,5},{5,4},{6,7},{7,6},{8,9},{9,8},{10,11... | collective-permute-start | bytes 6291464 | tf_op jit(solution)/shard_map/ppermute | solution.py:431
  184.4 22.4 %collective-permute-start.24 = (bf16[4,256,512]{2,1,0:T(8,128)(2,1)S(1)}, bf16[4,256,512]{2,1,0:T(8,128)(2,1)S(1)}, u32[]{:S(2)}, u32[]{:S(2)}) collective-permute-start(bf16[4,256,512]{2,1,0:T(8,128)(2,1)S(1)} %bitcast.105), channel_id=1, source_target_pairs={{0,4},{2,6},{4,0},{6,2},{8,12},{10,14},{12,8},{14,10},{16,20},{18,... | collective-permute-start | bytes 3145736 | tf_op jit(solution)/shard_map/ppermute | solution.py:428
  208.2 12.2 %collective-permute-start.25 = (bf16[4,128,512]{2,1,0:T(8,128)(2,1)}, bf16[4,128,512]{2,1,0:T(8,128)(2,1)S(1)}, u32[]{:S(2)}, u32[]{:S(2)}) collective-permute-start(bf16[4,128,512]{2,1,0:T(8,128)(2,1)} %bitcast.20), channel_id=1, source_target_pairs={{0,8},{2,10},{4,12},{6,14},{8,0},{10,2},{12,4},{14,6},{16,24},{18,... | collective-permute-start | bytes 1572872 | tf_op jit(solution)/shard_map/ppermute | solution.py:428
  220.6 10.0 %collective-permute-start.26 = (bf16[4,64,512]{2,1,0:T(8,128)(2,1)S(1)}, bf16[4,64,512]{2,1,0:T(8,128)(2,1)S(1)}, u32[]{:S(2)}, u32[]{:S(2)}) collective-permute-start(bf16[4,64,512]{2,1,0:T(8,128)(2,1)S(1)} %bitcast.112), channel_id=1, source_target_pairs={{0,16},{2,18},{4,20},{6,22},{8,24},{10,26},{12,28},{14,30},{16,0},... | collective-permute-start | bytes 786440 | tf_op jit(solution)/shard_map/ppermute | solution.py:428
  231.4 279.3 %all-gather.7.cloned.1.call-start = ((), (), s32[]{:S(2)}) async-start(), calls=%async_computation.1 | async-start | bytes 8912896 | tf_op jit(solution)/shard_map/all_gather | solution.py:612
  244.2 19.0 %collective-permute-start.5 = (bf16[128,2048]{1,0:T(8,128)(2,1)S(1)}, bf16[128,2048]{1,0:T(8,128)(2,1)}, u32[]{:S(2)}, u32[]{:S(2)}) collective-permute-start(bf16[128,2048]{1,0:T(8,128)(2,1)S(1)} %collective-permute-done.3.p0), channel_id=1, source_target_pairs={{0,8},{2,10},{4,12},{6,14},{8,0},{10,2},{12,4},{14,6},{16,24},{18,... | collective-permute-start | bytes 1572872 | tf_op jit(solution)/shard_map/ppermute | solution.py:428
  253.0 32.8 %collective-permute-start.6 = (bf16[128,2048]{1,0:T(8,128)(2,1)}, bf16[128,2048]{1,0:T(8,128)(2,1)}, u32[]{:S(2)}, u32[]{:S(2)}) collective-permute-start(bf16[128,2048]{1,0:T(8,128)(2,1)} %collective-permute-done.4.p1), channel_id=1, source_target_pairs={{0,8},{2,10},{4,12},{6,14},{8,0},{10,2},{12,4},{14,6},{16,24},{18,... | collective-permute-start | bytes 1572872 | tf_op jit(solution)/shard_map/ppermute | solution.py:428
  253.0 52.6 %collective-permute-start.7 = (bf16[256,1024]{1,0:T(8,128)(2,1)}, bf16[256,1024]{1,0:T(8,128)(2,1)}, u32[]{:S(2)}, u32[]{:S(2)}) collective-permute-start(bf16[256,1024]{1,0:T(8,128)(2,1)} %get-tuple-element.70), channel_id=1, source_target_pairs={{0,1},{1,0},{2,3},{3,2},{4,5},{5,4},{6,7},{7,6},{8,9},{9,8},{10,11... | collective-permute-start | bytes 1572872 | tf_op jit(solution)/shard_map/ppermute | solution.py:431
  304.0 50.2 %collective-permute-start.27 = (bf16[4,512,512]{2,1,0:T(8,128)(2,1)}, bf16[4,512,512]{2,1,0:T(8,128)(2,1)S(1)}, u32[]{:S(2)}, u32[]{:S(2)}) collective-permute-start(bf16[4,512,512]{2,1,0:T(8,128)(2,1)} %get-tuple-element.93), channel_id=1, source_target_pairs={{0,1},{1,0},{2,3},{3,2},{4,5},{5,4},{6,7},{7,6},{8,9},{9,8},{10,11... | collective-permute-start | bytes 6291464 | tf_op jit(solution)/shard_map/ppermute | solution.py:431
  305.6 9.4 %collective-permute-start.8 = (bf16[256,1024]{1,0:T(8,128)(2,1)}, bf16[256,1024]{1,0:T(8,128)(2,1)S(1)}, u32[]{:S(2)}, u32[]{:S(2)}) collective-permute-start(bf16[256,1024]{1,0:T(8,128)(2,1)} %collective-permute-done.7.d0), channel_id=1, source_target_pairs={{0,4},{2,6},{4,0},{6,2},{8,12},{10,14},{12,8},{14,10},{16,20},{18,... | collective-permute-start | bytes 1572872 | tf_op jit(solution)/shard_map/ppermute | solution.py:428
  306.3 31.0 %collective-permute-start.9 = (bf16[256,1024]{1,0:T(8,128)(2,1)}, bf16[256,1024]{1,0:T(8,128)(2,1)S(1)}, u32[]{:S(2)}, u32[]{:S(2)}) collective-permute-start(bf16[256,1024]{1,0:T(8,128)(2,1)} %collective-permute-done.7.d0), channel_id=1, source_target_pairs={{0,8},{2,10},{4,12},{6,14},{8,0},{10,2},{12,4},{14,6},{16,24},{18,... | collective-permute-start | bytes 1572872 | tf_op jit(solution)/shard_map/ppermute | solution.py:428
  315.0 22.3 %collective-permute-start.10 = (bf16[256,1024]{1,0:T(8,128)(2,1)S(1)}, bf16[256,1024]{1,0:T(8,128)(2,1)S(1)}, u32[]{:S(2)}, u32[]{:S(2)}) collective-permute-start(bf16[256,1024]{1,0:T(8,128)(2,1)S(1)} %collective-permute-done.8.d1), channel_id=1, source_target_pairs={{0,8},{2,10},{4,12},{6,14},{8,0},{10,2},{12,4},{14,6},{16,24},{18,... | collective-permute-start | bytes 1572872 | tf_op jit(solution)/shard_map/ppermute | solution.py:428
  337.0 27.3 %collective-permute-start.35 = (bf16[2,512,512]{2,1,0:T(8,128)(2,1)}, bf16[2,512,512]{2,1,0:T(8,128)(2,1)S(1)}, u32[]{:S(2)}, u32[]{:S(2)}) collective-permute-start(bf16[2,512,512]{2,1,0:T(8,128)(2,1)} %get-tuple-element.109), channel_id=1, source_target_pairs={{0,1},{1,0},{2,3},{3,2},{4,5},{5,4},{6,7},{7,6},{8,9},{9,8},{10,11... | collective-permute-start | bytes 3145736 | tf_op jit(solution)/shard_map/ppermute | solution.py:431
  352.4 23.1 %collective-permute-start.31 = (bf16[2,512,512]{2,1,0:T(8,128)(2,1)S(1)}, bf16[2,512,512]{2,1,0:T(8,128)(2,1)S(1)}, u32[]{:S(2)}, u32[]{:S(2)}) collective-permute-start(bf16[2,512,512]{2,1,0:T(8,128)(2,1)S(1)} %get-tuple-element.101), channel_id=1, source_target_pairs={{0,1},{1,0},{2,3},{3,2},{4,5},{5,4},{6,7},{7,6},{8,9},{9,8},{10,11... | collective-permute-start | bytes 3145736 | tf_op jit(solution)/shard_map/ppermute | solution.py:431
  354.7 22.3 %collective-permute-start.28 = (bf16[4,256,512]{2,1,0:T(8,128)(2,1)S(1)}, bf16[4,256,512]{2,1,0:T(8,128)(2,1)S(1)}, u32[]{:S(2)}, u32[]{:S(2)}) collective-permute-start(bf16[4,256,512]{2,1,0:T(8,128)(2,1)S(1)} %bitcast.104), channel_id=1, source_target_pairs={{0,4},{2,6},{4,0},{6,2},{8,12},{10,14},{12,8},{14,10},{16,20},{18,... | collective-permute-start | bytes 3145736 | tf_op jit(solution)/shard_map/ppermute | solution.py:428
  364.6 16.3 %collective-permute-start.36 = (bf16[2,256,512]{2,1,0:T(8,128)(2,1)S(1)}, bf16[2,256,512]{2,1,0:T(8,128)(2,1)S(1)}, u32[]{:S(2)}, u32[]{:S(2)}) collective-permute-start(bf16[2,256,512]{2,1,0:T(8,128)(2,1)S(1)} %bitcast.108), channel_id=1, source_target_pairs={{0,4},{2,6},{4,0},{6,2},{8,12},{10,14},{12,8},{14,10},{16,20},{18,... | collective-permute-start | bytes 1572872 | tf_op jit(solution)/shard_map/ppermute | solution.py:428
  375.8 10.6 %collective-permute-start.32 = (bf16[2,256,512]{2,1,0:T(8,128)(2,1)S(1)}, bf16[2,256,512]{2,1,0:T(8,128)(2,1)S(1)}, u32[]{:S(2)}, u32[]{:S(2)}) collective-permute-start(bf16[2,256,512]{2,1,0:T(8,128)(2,1)S(1)} %bitcast.107), channel_id=1, source_target_pairs={{0,4},{2,6},{4,0},{6,2},{8,12},{10,14},{12,8},{14,10},{16,20},{18,... | collective-permute-start | bytes 1572872 | tf_op jit(solution)/shard_map/ppermute | solution.py:428
  377.3 30.6 %collective-permute-start.29 = (bf16[4,128,512]{2,1,0:T(8,128)(2,1)S(1)}, bf16[4,128,512]{2,1,0:T(8,128)(2,1)S(1)}, u32[]{:S(2)}, u32[]{:S(2)}) collective-permute-start(bf16[4,128,512]{2,1,0:T(8,128)(2,1)S(1)} %bitcast.106), channel_id=1, source_target_pairs={{0,8},{2,10},{4,12},{6,14},{8,0},{10,2},{12,4},{14,6},{16,24},{18,... | collective-permute-start | bytes 1572872 | tf_op jit(solution)/shard_map/ppermute | solution.py:428
  381.0 12.6 %collective-permute-start.37 = (bf16[2,128,512]{2,1,0:T(8,128)(2,1)S(1)}, bf16[2,128,512]{2,1,0:T(8,128)(2,1)S(1)}, u32[]{:S(2)}, u32[]{:S(2)}) collective-permute-start(bf16[2,128,512]{2,1,0:T(8,128)(2,1)S(1)} %bitcast.110), channel_id=1, source_target_pairs={{0,8},{2,10},{4,12},{6,14},{8,0},{10,2},{12,4},{14,6},{16,24},{18,... | collective-permute-start | bytes 786440 | tf_op jit(solution)/shard_map/ppermute | solution.py:428
  386.6 18.6 %collective-permute-start.33 = (bf16[2,128,512]{2,1,0:T(8,128)(2,1)S(1)}, bf16[2,128,512]{2,1,0:T(8,128)(2,1)S(1)}, u32[]{:S(2)}, u32[]{:S(2)}) collective-permute-start(bf16[2,128,512]{2,1,0:T(8,128)(2,1)S(1)} %bitcast.111), channel_id=1, source_target_pairs={{0,8},{2,10},{4,12},{6,14},{8,0},{10,2},{12,4},{14,6},{16,24},{18,... | collective-permute-start | bytes 786440 | tf_op jit(solution)/shard_map/ppermute | solution.py:428
  393.7 15.8 %collective-permute-start.38 = (bf16[2,64,512]{2,1,0:T(8,128)(2,1)S(1)}, bf16[2,64,512]{2,1,0:T(8,128)(2,1)S(1)}, u32[]{:S(2)}, u32[]{:S(2)}) collective-permute-start(bf16[2,64,512]{2,1,0:T(8,128)(2,1)S(1)} %bitcast.113), channel_id=1, source_target_pairs={{0,16},{2,18},{4,20},{6,22},{8,24},{10,26},{12,28},{14,30},{16,0},... | collective-permute-start | bytes 393224 | tf_op jit(solution)/shard_map/ppermute | solution.py:428
  408.1 10.1 %collective-permute-start.30 = (bf16[4,64,512]{2,1,0:T(8,128)(2,1)S(1)}, bf16[4,64,512]{2,1,0:T(8,128)(2,1)S(1)}, u32[]{:S(2)}, u32[]{:S(2)}) collective-permute-start(bf16[4,64,512]{2,1,0:T(8,128)(2,1)S(1)} %bitcast.109), channel_id=1, source_target_pairs={{0,16},{2,18},{4,20},{6,22},{8,24},{10,26},{12,28},{14,30},{16,0},... | collective-permute-start | bytes 786440 | tf_op jit(solution)/shard_map/ppermute | solution.py:428
  451.5 11.4 %collective-permute-start.17 = (f32[512,1024]{1,0:T(8,128)}, f32[512,1024]{1,0:T(8,128)}, u32[]{:S(2)}, u32[]{:S(2)}) collective-permute-start(f32[512,1024]{1,0:T(8,128)} %get-tuple-element.79), channel_id=1, source_target_pairs={{0,2},{2,0},{4,6},{6,4},{8,10},{10,8},{12,14},{14,12},{16,18},{18,... | collective-permute-start | bytes 6291464 | tf_op jit(solution)/shard_map/ppermute | solution.py:428
  (59 other events, 341.6 us)
Sparse Core Ops, SparseCore 0:
  231.5 55.7 all-gather.4
  419.4 80.5 all-gather.6
